TPU v7x, 512 devices: a whole 4x4x16 slice. The times are simulated.
512 devices in a mesh: gx: 32 (over x_hi, z), gy: 16 (over y, x_lo, core).
Axes of the slice: x: 4 (x_hi: 2, x_lo: 2; x = x_hi * 2 + x_lo), y: 4, z: 16, core: 2. Of those that a mesh axis runs over, the one named last changes fastest.
Arguments:
- features: bfloat16 [32, 256, 6144], P(None, 'gx', 'gy'), may hold values from -6 to 6
- brick_list: int32 [32, 16, 6], P('gx', 'gy'), may hold values from -1 to 5, as said below
- weight_one: bfloat16 [3, 3, 3, 32, 32], replicated, may hold values from -0.21875 to 0.21875
- weight_two: bfloat16 [3, 3, 3, 32, 32], replicated, may hold values from -0.21875 to 0.21875
- cotangent: bfloat16 [32, 256, 6144], P(None, 'gx', 'gy'), may hold values from -6 to 6
Outputs:
- block_out: bfloat16 [32, 256, 6144], P(None, 'gx', 'gy')
- grad_features: bfloat16 [32, 256, 6144], P(None, 'gx', 'gy')
- grad_one: float32 [3, 3, 3, 32, 32], replicated
- grad_two: float32 [3, 3, 3, 32, 32], replicated
Inputs may be any that keep to these rules, and one draw needn't show every extreme that they name: `brick_list`: each device's row first names distinct local bricks (0 to 5), then -1 in the unused slots. Some device lists all of its bricks, some device lists only max(1, 1) of them.
All inputs are finite; a program needn't handle non-finite values.
Results may differ from a plain program's by a relative error of at most 0.003.
Values may be sent and summed in bfloat16 or wider, within the bound.
A program may use at most 128 MiB of HBM per device.

v0:
```python
import jax
import jax.numpy as jnp
from jax import lax
from jax.sharding import PartitionSpec as P

XB = 1
YB = 1
TBZ = 6
NB = 6


def padded_2(cells, sides, width):
    for axis, dim in sides:
        count = lax.axis_size(axis)
        ends = count - 1
        head = lax.slice_in_dim(cells, 0, width, axis=dim)
        tail = lax.slice_in_dim(cells, cells.shape[dim] - width, cells.shape[dim], axis=dim)
        cells = jnp.concatenate(
            [
                lax.ppermute(tail, axis, [(i, (i + 1) % count) for i in range(ends)]),
                cells,
                lax.ppermute(head, axis, [((i + 1) % count, i) for i in range(ends)]),
            ],
            axis=dim,
        )
    return cells


def local_occupancy(brick_list):
    hits = jax.nn.one_hot(brick_list.reshape(NB), NB, dtype=jnp.float32).sum(axis=0)
    hits = hits.reshape(XB, YB, TBZ)
    for axis_number in range(3):
        hits = jnp.repeat(hits, 8, axis=axis_number)
    return hits


def pad_depth(field):
    return jnp.pad(field, ((0, 0), (0, 0), (0, 0), (1, 1)))


def depth_stack(padded):
    depth = padded.shape[3] - 2
    return jnp.concatenate(
        [padded[:, :, :, offset : offset + depth] for offset in range(3)], axis=0
    )


def convolve(padded, weight):
    size_x = padded.shape[1] - 2
    size_y = padded.shape[2] - 2
    channels = weight.shape[3]
    stacked = depth_stack(padded)
    running = None
    for shift_x in range(3):
        for shift_y in range(3):
            window = stacked[:, shift_x : shift_x + size_x, shift_y : shift_y + size_y, :]
            kernel = weight[shift_x, shift_y].reshape(3 * channels, channels)
            product = jnp.einsum(
                "ixyz,io->oxyz", window, kernel, preferred_element_type=jnp.float32
            )
            running = product if running is None else running + product
    return running


def kernel_grad(padded, delta):
    size_x = delta.shape[1]
    size_y = delta.shape[2]
    channels = delta.shape[0]
    stacked = depth_stack(padded)
    planes = []
    for shift_x in range(3):
        rows_y = []
        for shift_y in range(3):
            window = stacked[:, shift_x : shift_x + size_x, shift_y : shift_y + size_y, :]
            product = jnp.einsum("ixyz,oxyz->io", window, delta, preferred_element_type=jnp.float32)
            rows_y.append(product.reshape(3, channels, channels))
        planes.append(jnp.stack(rows_y))
    return jnp.stack(planes)


def flipped(weight):
    return jnp.swapaxes(jnp.flip(weight, (0, 1, 2)), 3, 4)


def silu_slope(pre_value):
    sigma = jax.nn.sigmoid(pre_value)
    return sigma * (1.0 + pre_value * (1.0 - sigma))


def per_device(features, brick_list, weight_one, weight_two, cotangent):
    channels = features.shape[0]
    size_x = features.shape[1]
    depth_total = 8 * TBZ
    size_y = features.shape[2] // depth_total
    features = features.reshape(channels, size_x, size_y, depth_total)
    cotangent = cotangent.reshape(channels, size_x, size_y, depth_total)
    occupied = local_occupancy(brick_list)
    masked_in = (features.astype(jnp.float32) * occupied).astype(jnp.bfloat16)
    grad_masked = (cotangent.astype(jnp.float32) * occupied).astype(jnp.bfloat16)
    back_two = flipped(weight_two)
    back_one = flipped(weight_one)
    input_cycle = padded_2(masked_in, (("gx", 1), ("gy", 2)), 1)
    pre_one = occupied * convolve(pad_depth(input_cycle), weight_one)
    hidden = jax.nn.silu(pre_one).astype(jnp.bfloat16)
    hidden_cycle = padded_2(hidden, (("gx", 1), ("gy", 2)), 1)
    pre_two = occupied * convolve(pad_depth(hidden_cycle), weight_two)
    grad_cycle_in = padded_2(grad_masked, (("gx", 1), ("gy", 2)), 1)
    grad_hidden = convolve(pad_depth(grad_cycle_in), back_two)
    delta_own = (occupied * grad_hidden * silu_slope(pre_one)).astype(jnp.bfloat16)
    delta_cycle = padded_2(delta_own, (("gx", 1), ("gy", 2)), 1)
    grad_two = kernel_grad(pad_depth(hidden_cycle), grad_masked)
    grad_one = kernel_grad(pad_depth(input_cycle), delta_own)
    back = convolve(pad_depth(delta_cycle), back_one)
    block_out = (masked_in.astype(jnp.float32) + pre_two).astype(jnp.bfloat16)
    summed_one, summed_two = lax.psum((grad_one, grad_two), ("gx", "gy"))
    voxel_total = size_x * lax.axis_size("gx") * size_y * lax.axis_size("gy") * depth_total
    factor = float(voxel_total) ** (-0.5)
    grad_features = (occupied * (cotangent.astype(jnp.float32) + back)).astype(jnp.bfloat16)
    flat = (channels, size_x, size_y * depth_total)
    return (
        block_out.reshape(flat),
        grad_features.reshape(flat),
        summed_one * factor,
        summed_two * factor,
    )


def solution(mesh):
    return jax.shard_map(
        per_device,
        mesh=mesh,
        in_specs=(P(None, "gx", "gy"), P("gx", "gy", None), P(), P(), P(None, "gx", "gy")),
        out_specs=(P(None, "gx", "gy"), P(None, "gx", "gy"), P(), P()),
        check_vma=False,
    )
```

profile of v0, /device:TPU:1, one launch (start us, length us, event | category | flops | bytes accessed | tf_op | source)
XLA Modules:
  0.0 610.8 jit_solution(5972981152808993727)
XLA Ops:
  9.5 2.4 reshape.111
  11.8 2.5 multiply_convert_fusion
  15.6 5.0 collective-permute-start
  22.0 4.2 collective-permute-start.8
  35.0 8.7 %collective-permute-start.3 = (bf16[32,10,1,48]{3,0,2,1:T(8,128)(2,1)S(1)}, bf16[32,10,1,48]{3,0,2,1:T(8,128)(2,1)S(1)}, u32[]{:S(2)}, u32[]{:S(2)}) collective-permute-start(bf16[32,10,1,48]{3,0,2,1:T(8,128)(2,1)S(1)} %get-tuple-element.42), channel_id=1, source_target_pairs={{1,0},{2,1},{3,2},{4,3},{5,4},{6,5},{7,6},{8,7},{9,8},{10,9},{11,1... | collective-permute-start | bytes 92168 | tf_op jit(solution)/shard_map/ppermute | solution.py:22
  43.7 1.9 collective-permute-start.2
  45.7 2.4 collective-permute-start.11
  48.1 3.2 collective-permute-start.10
  71.0 4.0 collective-permute-start.4
  76.3 4.0 collective-permute-start.12
  81.2 2.3 collective-permute-start.7
  83.5 3.3 collective-permute-start.6
  86.8 1.9 collective-permute-start.15
  88.8 3.6 collective-permute-start.14
  94.5 3.1 fusion.236
  97.7 1.4 fusion.219
  101.8 1.5 fusion.225
  103.3 1.5 fusion.227
  107.5 1.4 fusion.233
  110.8 1.7 fusion.1
  127.9 5.6 fusion.164
  137.9 462.5 %all-reduce.7.cloned.1.call-done = (f32[3,3,3,32,32]{4,3,2,1,0:T(8,128)}, f32[3,3,3,32,32]{4,3,2,1,0:T(8,128)}) async-done(((f32[3,3,3,32,32]{4,3,2,1,0:T(8,128)}, f32[3,3,3,32,32]{4,3,2,1,0:T(8,128)}), (f32[3,3,3,32,32]{4,3,2,1,0:T(8,128)}, f32[3,3,3,32,32]{4,3,2,1,0:T(8,128)})) %all-reduce.7.cloned.1.call-update) | async-done | bytes 221200 | tf_op jit(solution)/shard_map/psum | solution.py:115
  600.4 1.8 broadcast_multiply_fusion.1
  602.2 1.8 broadcast_multiply_fusion
  (212 shorter events, 64.3 us)
Async XLA Ops:
  7.2 593.2 %all-reduce.7.cloned.1.call-start = ((), (), s32[]{:S(2)}) async-start(), calls=%async_computation | async-start | bytes 1769472 | tf_op jit(solution)/shard_map/psum | solution.py:115
  8.5 12.2 %copy-start.1 = (f32[32,8,8,48]{3,2,1,0:T(8,128)}, f32[32,8,8,48]{3,2,1,0:T(8,128)S(1)}, u32[]{:S(2)}) copy-start(f32[32,8,8,48]{3,2,1,0:T(8,128)S(1)} %reshape.112) | copy-start | bytes 1179652
  9.4 52.5 %copy-start.29 = (f32[48]{0:T(128)}, f32[48]{0:T(128)S(1)}, u32[]{:S(2)}) copy-start(f32[48]{0:T(128)S(1)} %broadcast_in_dim.10) | copy-start | bytes 580
  9.4 16.7 %copy-start.10 = (bf16[3,3,3,32,32]{4,3,2,1,0:T(8,128)(2,1)S(1)}, bf16[3,3,3,32,32]{4,3,2,1,0:T(8,128)(2,1)}, u32[]{:S(2)}) copy-start(bf16[3,3,3,32,32]{4,3,2,1,0:T(8,128)(2,1)} %param.8) | copy-start | bytes 165892
  11.8 15.0 %copy-start.11 = (bf16[3,3,3,32,32]{4,3,2,1,0:T(8,128)(2,1)S(1)}, bf16[3,3,3,32,32]{4,3,2,1,0:T(8,128)(2,1)}, u32[]{:S(2)}) copy-start(bf16[3,3,3,32,32]{4,3,2,1,0:T(8,128)(2,1)} %param.7) | copy-start | bytes 165892
  11.8 15.2 %copy-start.12 = (bf16[32,8,384]{2,1,0:T(8,128)(2,1)S(1)}, bf16[32,8,384]{2,1,0:T(8,128)(2,1)}, u32[]{:S(2)}) copy-start(bf16[32,8,384]{2,1,0:T(8,128)(2,1)} %param.9) | copy-start | bytes 589828
  14.3 20.6 %collective-permute-start.1 = (bf16[32,1,8,48]{3,0,2,1:T(8,128)(2,1)S(1)}, bf16[32,1,8,48]{3,0,2,1:T(8,128)(2,1)S(1)}, u32[]{:S(2)}, u32[]{:S(2)}) collective-permute-start(bf16[32,1,8,48]{3,0,2,1:T(8,128)(2,1)S(1)} %get-tuple-element.50), channel_id=1, source_target_pairs={{16,0},{32,16},{48,32},{64,48},{80,64},{96,80},{112,96},{128,112},... | collective-permute-start | bytes 73736 | tf_op jit(solution)/shard_map/ppermute | solution.py:22
  15.6 19.3 %collective-permute-start = (bf16[32,1,8,48]{3,0,2,1:T(8,128)(2,1)S(1)}, bf16[32,1,8,48]{3,0,2,1:T(8,128)(2,1)S(1)}, u32[]{:S(2)}, u32[]{:S(2)}) collective-permute-start(bf16[32,1,8,48]{3,0,2,1:T(8,128)(2,1)S(1)} %get-tuple-element.49), channel_id=1, source_target_pairs={{0,16},{16,32},{32,48},{48,64},{64,80},{80,96},{96,112},{112,128},... | collective-permute-start | bytes 73736 | tf_op jit(solution)/shard_map/ppermute | solution.py:20
  20.7 24.9 %collective-permute-start.9 = (bf16[32,1,8,48]{3,0,2,1:T(8,128)(2,1)S(1)}, bf16[32,1,8,48]{3,0,2,1:T(8,128)(2,1)S(1)}, u32[]{:S(2)}, u32[]{:S(2)}) collective-permute-start(bf16[32,1,8,48]{3,0,2,1:T(8,128)(2,1)S(1)} %get-tuple-element.46), channel_id=1, source_target_pairs={{16,0},{32,16},{48,32},{64,48},{80,64},{96,80},{112,96},{128,112},... | collective-permute-start | bytes 73736 | tf_op jit(solution)/shard_map/ppermute | solution.py:22
  22.0 23.7 %collective-permute-start.8 = (bf16[32,1,8,48]{3,0,2,1:T(8,128)(2,1)S(1)}, bf16[32,1,8,48]{3,0,2,1:T(8,128)(2,1)S(1)}, u32[]{:S(2)}, u32[]{:S(2)}) collective-permute-start(bf16[32,1,8,48]{3,0,2,1:T(8,128)(2,1)S(1)} %get-tuple-element.45), channel_id=1, source_target_pairs={{0,16},{16,32},{32,48},{48,64},{64,80},{80,96},{96,112},{112,128},... | collective-permute-start | bytes 73736 | tf_op jit(solution)/shard_map/ppermute | solution.py:20
  35.0 16.3 %collective-permute-start.3 = (bf16[32,10,1,48]{3,0,2,1:T(8,128)(2,1)S(1)}, bf16[32,10,1,48]{3,0,2,1:T(8,128)(2,1)S(1)}, u32[]{:S(2)}, u32[]{:S(2)}) collective-permute-start(bf16[32,10,1,48]{3,0,2,1:T(8,128)(2,1)S(1)} %get-tuple-element.42), channel_id=1, source_target_pairs={{1,0},{2,1},{3,2},{4,3},{5,4},{6,5},{7,6},{8,7},{9,8},{10,9},{11,1... | collective-permute-start | bytes 92168 | tf_op jit(solution)/shard_map/ppermute | solution.py:22
  43.7 7.6 %collective-permute-start.2 = (bf16[32,10,1,48]{3,0,2,1:T(8,128)(2,1)S(1)}, bf16[32,10,1,48]{3,0,2,1:T(8,128)(2,1)S(1)}, u32[]{:S(2)}, u32[]{:S(2)}) collective-permute-start(bf16[32,10,1,48]{3,0,2,1:T(8,128)(2,1)S(1)} %get-tuple-element.41), channel_id=1, source_target_pairs={{0,1},{1,2},{2,3},{3,4},{4,5},{5,6},{6,7},{7,8},{8,9},{9,10},{10,1... | collective-permute-start | bytes 92168 | tf_op jit(solution)/shard_map/ppermute | solution.py:20
  45.7 10.6 %collective-permute-start.11 = (bf16[32,10,1,48]{3,0,2,1:T(8,128)(2,1)S(1)}, bf16[32,10,1,48]{3,0,2,1:T(8,128)(2,1)S(1)}, u32[]{:S(2)}, u32[]{:S(2)}) collective-permute-start(bf16[32,10,1,48]{3,0,2,1:T(8,128)(2,1)S(1)} %get-tuple-element.38), channel_id=1, source_target_pairs={{1,0},{2,1},{3,2},{4,3},{5,4},{6,5},{7,6},{8,7},{9,8},{10,9},{11,1... | collective-permute-start | bytes 92168 | tf_op jit(solution)/shard_map/ppermute | solution.py:22
  48.1 8.2 %collective-permute-start.10 = (bf16[32,10,1,48]{3,0,2,1:T(8,128)(2,1)S(1)}, bf16[32,10,1,48]{3,0,2,1:T(8,128)(2,1)S(1)}, u32[]{:S(2)}, u32[]{:S(2)}) collective-permute-start(bf16[32,10,1,48]{3,0,2,1:T(8,128)(2,1)S(1)} %get-tuple-element.37), channel_id=1, source_target_pairs={{0,1},{1,2},{2,3},{3,4},{4,5},{5,6},{6,7},{7,8},{8,9},{9,10},{10,1... | collective-permute-start | bytes 92168 | tf_op jit(solution)/shard_map/ppermute | solution.py:20
  69.7 11.5 %collective-permute-start.5 = (bf16[32,1,8,48]{3,0,2,1:T(8,128)(2,1)S(1)}, bf16[32,1,8,48]{3,0,2,1:T(8,128)(2,1)S(1)}, u32[]{:S(2)}, u32[]{:S(2)}) collective-permute-start(bf16[32,1,8,48]{3,0,2,1:T(8,128)(2,1)S(1)} %get-tuple-element.48), channel_id=1, source_target_pairs={{16,0},{32,16},{48,32},{64,48},{80,64},{96,80},{112,96},{128,112},... | collective-permute-start | bytes 73736 | tf_op jit(solution)/shard_map/ppermute | solution.py:22
  71.0 10.2 %collective-permute-start.4 = (bf16[32,1,8,48]{3,0,2,1:T(8,128)(2,1)S(1)}, bf16[32,1,8,48]{3,0,2,1:T(8,128)(2,1)S(1)}, u32[]{:S(2)}, u32[]{:S(2)}) collective-permute-start(bf16[32,1,8,48]{3,0,2,1:T(8,128)(2,1)S(1)} %get-tuple-element.47), channel_id=1, source_target_pairs={{0,16},{16,32},{32,48},{48,64},{64,80},{80,96},{96,112},{112,128},... | collective-permute-start | bytes 73736 | tf_op jit(solution)/shard_map/ppermute | solution.py:20
  75.0 11.8 %collective-permute-start.13 = (bf16[32,1,8,48]{3,0,2,1:T(8,128)(2,1)S(1)}, bf16[32,1,8,48]{3,0,2,1:T(8,128)(2,1)S(1)}, u32[]{:S(2)}, u32[]{:S(2)}) collective-permute-start(bf16[32,1,8,48]{3,0,2,1:T(8,128)(2,1)S(1)} %get-tuple-element.44), channel_id=1, source_target_pairs={{16,0},{32,16},{48,32},{64,48},{80,64},{96,80},{112,96},{128,112},... | collective-permute-start | bytes 73736 | tf_op jit(solution)/shard_map/ppermute | solution.py:22
  76.3 10.5 %collective-permute-start.12 = (bf16[32,1,8,48]{3,0,2,1:T(8,128)(2,1)S(1)}, bf16[32,1,8,48]{3,0,2,1:T(8,128)(2,1)S(1)}, u32[]{:S(2)}, u32[]{:S(2)}) collective-permute-start(bf16[32,1,8,48]{3,0,2,1:T(8,128)(2,1)S(1)} %get-tuple-element.43), channel_id=1, source_target_pairs={{0,16},{16,32},{32,48},{48,64},{64,80},{80,96},{96,112},{112,128},... | collective-permute-start | bytes 73736 | tf_op jit(solution)/shard_map/ppermute | solution.py:20
  81.2 11.2 %collective-permute-start.7 = (bf16[32,10,1,48]{3,0,2,1:T(8,128)(2,1)S(1)}, bf16[32,10,1,48]{3,0,2,1:T(8,128)(2,1)S(1)}, u32[]{:S(2)}, u32[]{:S(2)}) collective-permute-start(bf16[32,10,1,48]{3,0,2,1:T(8,128)(2,1)S(1)} %get-tuple-element.40), channel_id=1, source_target_pairs={{1,0},{2,1},{3,2},{4,3},{5,4},{6,5},{7,6},{8,7},{9,8},{10,9},{11,1... | collective-permute-start | bytes 92168 | tf_op jit(solution)/shard_map/ppermute | solution.py:22
  83.5 9.0 %collective-permute-start.6 = (bf16[32,10,1,48]{3,0,2,1:T(8,128)(2,1)S(1)}, bf16[32,10,1,48]{3,0,2,1:T(8,128)(2,1)S(1)}, u32[]{:S(2)}, u32[]{:S(2)}) collective-permute-start(bf16[32,10,1,48]{3,0,2,1:T(8,128)(2,1)S(1)} %get-tuple-element.39), channel_id=1, source_target_pairs={{0,1},{1,2},{2,3},{3,4},{4,5},{5,6},{6,7},{7,8},{8,9},{9,10},{10,1... | collective-permute-start | bytes 92168 | tf_op jit(solution)/shard_map/ppermute | solution.py:20
  86.8 22.0 %collective-permute-start.15 = (bf16[32,10,1,48]{3,0,2,1:T(8,128)(2,1)S(1)}, bf16[32,10,1,48]{3,0,2,1:T(8,128)(2,1)S(1)}, u32[]{:S(2)}, u32[]{:S(2)}) collective-permute-start(bf16[32,10,1,48]{3,0,2,1:T(8,128)(2,1)S(1)} %get-tuple-element.36), channel_id=1, source_target_pairs={{1,0},{2,1},{3,2},{4,3},{5,4},{6,5},{7,6},{8,7},{9,8},{10,9},{11,1... | collective-permute-start | bytes 92168 | tf_op jit(solution)/shard_map/ppermute | solution.py:22
  88.8 20.1 %collective-permute-start.14 = (bf16[32,10,1,48]{3,0,2,1:T(8,128)(2,1)S(1)}, bf16[32,10,1,48]{3,0,2,1:T(8,128)(2,1)S(1)}, u32[]{:S(2)}, u32[]{:S(2)}) collective-permute-start(bf16[32,10,1,48]{3,0,2,1:T(8,128)(2,1)S(1)} %get-tuple-element.35), channel_id=1, source_target_pairs={{0,1},{1,2},{2,3},{3,4},{4,5},{5,6},{6,7},{7,8},{8,9},{9,10},{10,1... | collective-permute-start | bytes 92168 | tf_op jit(solution)/shard_map/ppermute | solution.py:20
  110.7 9.7 %copy-start = (bf16[96,10,10,48]{3,0,2,1:T(8,128)(2,1)}, bf16[96,10,10,48]{3,0,2,1:T(8,128)(2,1)S(1)}, u32[]{:S(2)}) copy-start(bf16[96,10,10,48]{3,0,2,1:T(8,128)(2,1)S(1)} %pad_maximum_fusion.3) | copy-start | bytes 2764804
  127.9 6.6 %copy-start.9 = (f32[8,8,48,32]{2,3,1,0:T(8,128)S(1)}, f32[8,8,48,32]{2,3,1,0:T(8,128)}, u32[]{:S(2)}) copy-start(f32[8,8,48,32]{2,3,1,0:T(8,128)} %fusion.233) | copy-start | bytes 1179652
  (24 other events, 81.6 us)
Sparse Core Ops, SparseCore 0:
  128.0 472.3 all-reduce.6
where the time goes:
time: 612 us; the launch traced here: 611 us
  waiting for transfers between devices  463 us (76%)
  starting transfers between devices  49.7 us (8%)
  matrix products  48.2 us (8%)
  local copies, waits for them, and re-layouts  20.4 us (3%)
  other arithmetic  15.1 us (2%)
  between operations  15 us (2%)
    psum x1, waiting for transfers between devices, per_device(): summed_one, summed_two = lax.psum((grad_one, grad_two), ('gx', 'gy'))  462 us
    dot_general x36, matrix products, convolve(): jnp.einsum('ixyz,io->oxyz', window, kernel, preferred_element_type=jnp.fl...  36.5 us
    ppermute x8, starting transfers between devices, padded_2(): lax.ppermute(tail, axis, [(i, (i + 1) % count) for i in range(ends)])  29.2 us
    ppermute x8, starting transfers between devices, padded_2(): lax.ppermute(head, axis, [((i + 1) % count, i) for i in range(ends)])  20.5 us
  transfers between devices with their start and end apart: 17, of which 1 were waited for; matrix products, arithmetic and copies ran while one was open for 7% of the time, Pallas kernels for 0%

commit v1 on v0

v1 whole, which is shorter than its diff:
```python
import functools

import jax
import jax.numpy as jnp
from jax import lax
from jax.experimental import pallas as pl
from jax.experimental.pallas import tpu as pltpu
from jax.sharding import PartitionSpec as P

C = 32
SIDE = 8
NZ = 48
BRICKS = 6
LANES = SIDE * C
OWN = SIDE * NZ
ALL = OWN + 2 * NZ
PACKED = 512
X_HI = 2
MESH = pl.DeviceIdType.MESH
F32 = jnp.float32
BF16 = jnp.bfloat16


def dot(a, b, contract=((1,), (0,))):
    return lax.dot_general(a, b, (contract, ((), ())), preferred_element_type=F32)


def rows_mask(zero_at):
    z = lax.broadcasted_iota(jnp.int32, (NZ, LANES), 0)
    return jnp.concatenate([jnp.where(z == zero_at, 0.0, 1.0).astype(F32)] * SIDE, axis=0)


def from_below(value):
    return pltpu.roll(value, 1, 0) * rows_mask(0)


def from_above(value):
    return pltpu.roll(value, OWN - 1, 0) * rows_mask(NZ - 1)


def at(kx, ky, kz):
    return kx * 9 + ky * 3 + kz


def lane_block(shape=(C, 128)):
    return lax.broadcasted_iota(jnp.int32, shape, 1) // C


def widen_weights(w_ref, quad, which):
    lane = lax.broadcasted_iota(jnp.int32, (C, 128), 1)
    row = lax.broadcasted_iota(jnp.int32, (C, 128), 0)
    repeat = jnp.where(lane % C == row, 1.0, 0.0).astype(BF16)
    quad[which] = dot(w_ref[...], repeat).astype(BF16).reshape(27, C, 128)


def build_bands(quad, band, rim_in, rim_out):
    blocks = lane_block()
    masks = [jnp.where(blocks == b, 1.0, 0.0).astype(BF16) for b in range(4)]
    zero = jnp.zeros((C, 128), BF16)

    def step(i, carry):
        w, ky = i // 3, lax.rem(i, 3)
        rim_in[w, ky] = jnp.zeros((128, 3 * LANES), BF16)
        rim_out[w, ky] = jnp.zeros((LANES, 3 * 128), BF16)
        for kz in range(3):
            parts = [quad[w, at(kx, ky, kz)] for kx in range(3)]
            for xi in range(SIDE):
                for tile in range(2):
                    value = None
                    for kx in range(3):
                        xo = xi + 1 - kx - 4 * tile
                        if 0 <= xo < 4:
                            term = parts[kx] * masks[xo]
                            value = term if value is None else value + term
                    lanes = pl.ds(kz * LANES + tile * 128, 128)
                    band[w, ky, pl.ds(xi * C, C), lanes] = zero if value is None else value
            rim_in[w, ky, pl.ds(0, C), pl.ds(kz * LANES, 128)] = parts[0] * masks[0]
            rim_in[w, ky, pl.ds(C, C), pl.ds(kz * LANES + 128, 128)] = parts[2] * masks[3]
            rim_out[w, ky, pl.ds(0, C), pl.ds(kz * 128, 128)] = parts[2] * masks[2]
            rim_out[w, ky, pl.ds(LANES - C, C), pl.ds(kz * 128, 128)] = parts[0] * masks[3]
        return carry

    lax.fori_loop(0, 6, step, 0)


def shifted_rows(cells, rim, field):
    parts = [cells[field, pl.ds(ky * NZ, OWN), :] for ky in range(3)]
    return jnp.concatenate(parts + [rim[pl.ds(ky * NZ, OWN), :] for ky in range(3)], axis=1)


def conv_forward(cells, rim, band, rim_in, w):
    lhs = shifted_rows(cells, rim, 0)
    terms = []
    for kz in range(3):
        lanes = pl.ds(kz * LANES, LANES)
        rhs = jnp.concatenate(
            [band[w, ky, :, lanes] for ky in range(3)]
            + [rim_in[w, ky, :, lanes] for ky in range(3)],
            axis=0,
        )
        terms.append(dot(lhs, rhs))
    return terms[1] + from_below(terms[0]) + from_above(terms[2])


def conv_backward(cells, rim, band, rim_out, w):
    lhs = shifted_rows(cells, rim, 1)
    terms = []
    for kz in range(3):
        back = 2 - kz
        rhs = jnp.concatenate(
            [band[w, 2 - ky, :, pl.ds(back * LANES, LANES)] for ky in range(3)]
            + [rim_out[w, 2 - ky, :, pl.ds(back * 128, 128)] for ky in range(3)],
            axis=1,
        )
        terms.append(dot(lhs, rhs, ((1,), (1,))))
    return terms[1] + from_below(terms[0]) + from_above(terms[2])


def kernel_sums(own, cells, rim, field):
    wide = own.astype(F32)
    turned = {
        -1: from_above(wide).astype(BF16).T,
        0: own.T,
        1: from_below(wide).astype(BF16).T,
    }
    tall = jnp.concatenate([turned[sz] for sz in (-1, 0, 1)], axis=0)
    ends = jnp.concatenate(
        [turned[sz][part] for sz in (-1, 0, 1) for part in (slice(0, C), slice(LANES - C, LANES))],
        axis=0,
    )
    blocks = lane_block()
    sums = {}
    for sy in (-1, 0, 1):
        rows = pl.ds((1 + sy) * NZ, OWN)
        main = dot(tall, cells[field, rows, :])
        edge = dot(ends, rim[rows, :])
        for n, sz in enumerate((-1, 0, 1)):
            for sx in (-1, 0, 1):
                halves = []
                for tile in range(2):
                    value = None
                    for b in range(4):
                        a = 4 * tile + b - sx
                        if 0 <= a < SIDE:
                            top = n * LANES + a * C
                            term = main[top : top + C, tile * 128 : tile * 128 + 128]
                        else:
                            term = jnp.zeros((C, 128), F32)
                        value = term if value is None else jnp.where(blocks >= b, term, value)
                    halves.append(value)
                total = halves[0] + halves[1]
                if sx == -1:
                    total = total + jnp.where(blocks == 2 * field, edge[n * 64 : n * 64 + C], 0.0)
                if sx == 1:
                    total = total + jnp.where(
                        blocks == 2 * field + 1, edge[n * 64 + C : n * 64 + 64], 0.0
                    )
                sums[sx, sy, sz] = total
    return sums


def fold_four(a, b, c, d):
    blocks = lane_block()
    low = blocks < 2
    middle = (blocks == 1) | (blocks == 2)
    even = (blocks == 0) | (blocks == 2)
    ac = jnp.where(low, a, c) + pltpu.roll(jnp.where(low, c, a), 64, 1)
    bd = jnp.where(middle, b, d) + pltpu.roll(jnp.where(middle, d, b), 64, 1)
    return jnp.where(even, ac, bd) + pltpu.roll(jnp.where(even, bd, ac), 96, 1)


def kernel(
    n_gx, n_gy, factor,
    list_ref, f_ref, g_ref, w1_ref, w2_ref,
    block_ref, back_ref, one_ref, two_ref,
    turned_a, cells_a, side_a, corner_a, rim_a,
    turned_b, cells_b, side_b, corner_b, rim_b,
    quad, band, rim_in, rim_out,
    packed, gathered, column, total,
    halo_send_a, halo_recv_a, halo_send_b, halo_recv_b,
    part_send, part_recv, line_send, line_recv, full_send, full_recv,
):
    gx, gy = lax.axis_index("gx"), lax.axis_index("gy")
    n_line = n_gx // X_HI
    n_plane = X_HI * n_gy
    x_hi, line = gx // n_line, lax.rem(gx, n_line)
    rank = x_hi * n_gy + gy
    share = PACKED // n_plane

    def beside(dx, dy):
        return (lax.rem(gx + dx + n_gx, n_gx), lax.rem(gy + dy + n_gy, n_gy))

    def in_plane(other):
        return (other // n_gy * n_line + line, lax.rem(other, n_gy))

    def in_line(other):
        return (x_hi * n_line + other, gy)

    barrier = pltpu.get_barrier_semaphore()
    around = [(dx, dy) for dx in (-1, 0, 1) for dy in (-1, 0, 1) if (dx, dy) != (0, 0)]
    for dx, dy in around:
        pl.semaphore_signal(barrier, inc=1, device_id=beside(dx, dy), device_id_type=MESH)

    def greet_plane(d, carry):
        target = in_plane(lax.rem(rank + d, n_plane))
        pl.semaphore_signal(barrier, inc=1, device_id=target, device_id_type=MESH)
        return carry

    def greet_line(d, carry):
        target = in_line(lax.rem(line + d, n_line))
        pl.semaphore_signal(barrier, inc=1, device_id=target, device_id_type=MESH)
        return carry

    lax.fori_loop(1, n_plane, greet_plane, 0)
    lax.fori_loop(1, n_line, greet_line, 0)

    hits = []
    for brick in range(BRICKS):
        count = jnp.int32(0)
        for slot in range(BRICKS):
            count = count + jnp.where(list_ref[0, 0, slot] == brick, 1, 0)
        hits.append(count.astype(F32))
    occupied = jnp.concatenate(
        [jnp.full((8, LANES), hit, F32) for hit in hits] * SIDE, axis=0
    )
    brick_of = lax.rem(lax.broadcasted_iota(jnp.int32, (8, OWN), 1), NZ) // 8
    across = jnp.zeros((8, OWN), F32)
    for brick in range(BRICKS):
        across = across + jnp.where(brick_of == brick, hits[brick], 0.0)
    across = jnp.concatenate([across] * (LANES // 8), axis=0)

    row = lax.broadcasted_iota(jnp.int32, (LANES, LANES), 0)
    col = lax.broadcasted_iota(jnp.int32, (LANES, LANES), 1)
    order = jnp.where(col == (row % C) * SIDE + row // C, 1.0, 0.0).astype(BF16)
    reorder = jnp.where(row == (col % C) * SIDE + col // C, 1.0, 0.0).astype(BF16)
    for field, ref in enumerate((f_ref, g_ref)):
        value = (dot(order, ref[...]) * across).astype(BF16)
        turned_a[field] = value
        cells_a[field, pl.ds(NZ, OWN), :] = value.T

    pl.semaphore_wait(barrier, len(around) + n_plane - 1 + n_line - 1)

    def exchange(turned, cells, side, corner, send, recv):
        low, high = pl.ds(0, C), pl.ds(LANES - C, C)
        every, head, tail = pl.ds(0, OWN), pl.ds(0, 128), pl.ds(OWN - 128, 128)

        def strip(rows, lanes):
            return turned.at[:, rows, lanes]

        def slab(y):
            return cells.at[:, pl.ds((y + 1) * NZ, NZ), :]

        plan = [
            (slab(SIDE - 1), slab(-1), (0, 1)),
            (slab(0), slab(SIDE), (0, -1)),
            (strip(high, every), side.at[0], (1, 0)),
            (strip(low, every), side.at[1], (-1, 0)),
            (strip(high, tail), corner.at[0], (1, 1)),
            (strip(low, tail), corner.at[1], (-1, 1)),
            (strip(high, head), corner.at[2], (1, -1)),
            (strip(low, head), corner.at[3], (-1, -1)),
        ]
        copies = []
        for n, (src, dst, (dx, dy)) in enumerate(plan):
            copies.append(
                pltpu.make_async_remote_copy(
                    src_ref=src,
                    dst_ref=dst,
                    send_sem=send.at[n],
                    recv_sem=recv.at[n],
                    device_id=beside(dx, dy),
                    device_id_type=MESH,
                )
            )
        for copy in copies:
            copy.start()
        return copies

    def edge(condition):
        return jnp.where(condition, 1.0, 0.0).astype(F32)

    def place_rims(copies, cells, side, corner, rim):
        for copy in copies:
            copy.wait_recv()
        first_y, last_y = edge(gy > 0), edge(gy < n_gy - 1)
        first_x, last_x = edge(gx > 0), edge(gx < n_gx - 1)
        for rows, keep in ((pl.ds(0, NZ), first_y), (pl.ds(ALL - NZ, NZ), last_y)):
            for field in range(2):
                cells[field, rows, :] = (cells[field, rows, :].astype(F32) * keep).astype(BF16)
        odd = lax.rem(lane_block((1, 128)), 2) == 1
        keep_x = jnp.where(odd, last_x, first_x)

        def turn(left, right):
            parts = [left[0], right[0], left[1], right[1]]
            return jnp.concatenate(parts, axis=0).T.astype(F32) * keep_x

        rim[pl.ds(NZ, OWN), :] = turn(side[0], side[1]).astype(BF16)
        upper = turn(corner[0], corner[1])[128 - NZ :] * first_y
        lower = turn(corner[2], corner[3])[:NZ] * last_y
        rim[pl.ds(0, NZ), :] = upper.astype(BF16)
        rim[pl.ds(ALL - NZ, NZ), :] = lower.astype(BF16)

    copies_a = exchange(turned_a, cells_a, side_a, corner_a, halo_send_a, halo_recv_a)
    widen_weights(w1_ref, quad, 0)
    widen_weights(w2_ref, quad, 1)
    build_bands(quad, band, rim_in, rim_out)
    place_rims(copies_a, cells_a, side_a, corner_a, rim_a)

    pre_one = conv_forward(cells_a, rim_a, band, rim_in, 0) * occupied
    sigma = jax.nn.sigmoid(pre_one)
    hidden = (pre_one * sigma).astype(BF16)
    slope = occupied * sigma * (1.0 + pre_one * (1.0 - sigma))
    delta = (conv_backward(cells_a, rim_a, band, rim_out, 1) * slope).astype(BF16)
    for field, value in enumerate((hidden, delta)):
        cells_b[field, pl.ds(NZ, OWN), :] = value
        turned_b[field] = value.T
    copies_b = exchange(turned_b, cells_b, side_b, corner_b, halo_send_b, halo_recv_b)

    sums_two = kernel_sums(hidden, cells_a, rim_a, 1)
    sums_one = kernel_sums(delta, cells_a, rim_a, 0)
    offsets = [(kx, ky, kz) for kx in (-1, 0, 1) for ky in (-1, 0, 1) for kz in (-1, 0, 1)]
    one = [sums_one[k] for k in offsets] + [jnp.zeros((C, 128), F32)]
    two = [sums_two[-k[0], -k[1], -k[2]] for k in offsets] + [jnp.zeros((C, 128), F32)]
    for n, start in enumerate(range(0, 28, 4)):
        packed[pl.ds(n * C, C), :] = fold_four(*one[start : start + 4])
        packed[pl.ds((7 + n) * C, C), :] = fold_four(*two[start : start + 4])
    packed[pl.ds(14 * C, PACKED - 14 * C), :] = jnp.zeros((PACKED - 14 * C, 128), F32)

    def share_of(ref, other):
        return ref.at[pl.ds(pl.multiple_of(other * share, share), share), :]

    def part_copy(target, source):
        return pltpu.make_async_remote_copy(
            src_ref=share_of(packed, target),
            dst_ref=gathered.at[source],
            send_sem=part_send.at[target],
            recv_sem=part_recv.at[source],
            device_id=in_plane(target),
            device_id_type=MESH,
        )

    def line_copy(target, source):
        return pltpu.make_async_remote_copy(
            src_ref=column.at[line],
            dst_ref=column.at[source],
            send_sem=line_send.at[target],
            recv_sem=line_recv.at[source],
            device_id=in_line(target),
            device_id_type=MESH,
        )

    def full_copy(target, source):
        return pltpu.make_async_remote_copy(
            src_ref=share_of(total, rank),
            dst_ref=share_of(total, source),
            send_sem=full_send.at[target],
            recv_sem=full_recv.at[source],
            device_id=in_plane(target),
            device_id_type=MESH,
        )

    def each(make, me, count, act):
        def step(d, carry):
            act(make, me, lax.rem(me + d, count))
            return carry

        lax.fori_loop(1, count, step, 0)

    def start(make, me, other):
        make(other, me).start()

    def landed(make, me, other):
        make(other, other).wait_recv()

    def sent(make, me, other):
        make(other, me).wait_send()

    def summed(ref, count):
        value = ref[0]
        for n in range(1, count):
            value = value + ref[n]
        return value

    each(part_copy, rank, n_plane, start)
    gathered[rank] = packed[pl.ds(pl.multiple_of(rank * share, share), share), :]

    place_rims(copies_b, cells_b, side_b, corner_b, rim_b)
    pre_two = conv_forward(cells_b, rim_b, band, rim_in, 1) * occupied
    middle = pl.ds(NZ, OWN)
    block_out = (cells_a[0, middle, :].astype(F32) + pre_two).astype(BF16)
    block_ref[...] = dot(reorder, block_out, ((1,), (1,))).astype(BF16)

    each(part_copy, rank, n_plane, landed)
    column[line] = summed(gathered, n_plane)
    each(line_copy, line, n_line, start)

    back = conv_backward(cells_b, rim_b, band, rim_out, 0) * occupied
    grad_features = (cells_a[1, middle, :].astype(F32) + back).astype(BF16)
    back_ref[...] = dot(reorder, grad_features, ((1,), (1,))).astype(BF16)

    each(line_copy, line, n_line, landed)
    total[pl.ds(pl.multiple_of(rank * share, share), share), :] = summed(column, n_line)
    each(full_copy, rank, n_plane, start)
    for copy in copies_a + copies_b:
        copy.wait_send()
    each(part_copy, rank, n_plane, sent)
    each(line_copy, line, n_line, sent)
    each(full_copy, rank, n_plane, landed)

    for n, first in enumerate(range(0, 27, 4)):
        count = min(4, 27 - first)
        one_ref[pl.ds(first * C, count * C), :] = (
            total[pl.ds(n * C, C), :].T[: count * C] * factor
        )
        group = total[pl.ds((7 + n) * C, C), :] * factor
        for k in range(count):
            two_ref[pl.ds((first + k) * C, C), :] = group[:, k * C : (k + 1) * C]
    each(full_copy, rank, n_plane, sent)


def per_device(features, brick_list, weight_one, weight_two, cotangent):
    n_gx, n_gy = lax.axis_size("gx"), lax.axis_size("gy")
    n_line, n_plane = n_gx // X_HI, X_HI * n_gy
    share = PACKED // n_plane
    factor = float(n_gx * SIDE * n_gy * SIDE * NZ) ** (-0.5)
    vmem = pl.BlockSpec(memory_space=pltpu.VMEM)
    halo = [
        pltpu.VMEM((2, LANES, OWN), BF16),
        pltpu.VMEM((2, ALL, LANES), BF16),
        pltpu.VMEM((2, 2, C, OWN), BF16),
        pltpu.VMEM((4, 2, C, 128), BF16),
        pltpu.VMEM((ALL, 128), BF16),
    ]
    block_out, grad_features, one, two = pl.pallas_call(
        functools.partial(kernel, n_gx, n_gy, factor),
        out_shape=(
            jax.ShapeDtypeStruct((LANES, OWN), BF16),
            jax.ShapeDtypeStruct((LANES, OWN), BF16),
            jax.ShapeDtypeStruct((27 * C, C), F32),
            jax.ShapeDtypeStruct((27 * C, C), F32),
        ),
        in_specs=[pl.BlockSpec(memory_space=pltpu.SMEM)] + [vmem] * 4,
        out_specs=[vmem] * 4,
        scratch_shapes=halo
        + halo
        + [
            pltpu.VMEM((2, 27, C, 128), BF16),
            pltpu.VMEM((2, 3, LANES, 3 * LANES), BF16),
            pltpu.VMEM((2, 3, 128, 3 * LANES), BF16),
            pltpu.VMEM((2, 3, LANES, 3 * 128), BF16),
            pltpu.VMEM((PACKED, 128), F32),
            pltpu.VMEM((n_plane, share, 128), F32),
            pltpu.VMEM((n_line, share, 128), F32),
            pltpu.VMEM((PACKED, 128), F32),
        ]
        + [pltpu.SemaphoreType.DMA((8,))] * 4
        + [pltpu.SemaphoreType.DMA((n_plane,))] * 2
        + [pltpu.SemaphoreType.DMA((n_line,))] * 2
        + [pltpu.SemaphoreType.DMA((n_plane,))] * 2,
        compiler_params=pltpu.CompilerParams(
            collective_id=0, has_side_effects=True, vmem_limit_bytes=48 * 1024 * 1024
        ),
    )(
        brick_list,
        features.reshape(LANES, OWN),
        cotangent.reshape(LANES, OWN),
        weight_one.reshape(27 * C, C),
        weight_two.reshape(27 * C, C),
    )
    flat = (C, SIDE, OWN)
    cube = (3, 3, 3, C, C)
    return block_out.reshape(flat), grad_features.reshape(flat), one.reshape(cube), two.reshape(cube)


def solution(mesh):
    return jax.shard_map(
        per_device,
        mesh=mesh,
        in_specs=(P(None, "gx", "gy"), P("gx", "gy", None), P(), P(), P(None, "gx", "gy")),
        out_specs=(P(None, "gx", "gy"), P(None, "gx", "gy"), P(), P()),
        check_vma=False,
    )
```

time: 612 us -> 58.4 us (0.10)
  waiting for transfers between devices: 463 us -> 0 us
  Pallas kernels: 0 us -> 50.3 us
  starting transfers between devices: 49.7 us -> 0 us
  matrix products: 48.2 us -> 0 us
  other arithmetic: 15.1 us -> 0 us
  between operations: 15 us -> 0.65 us
  local copies, waits for them, and re-layouts: 20.4 us -> 7.25 us
    psum x1 -> x0, waiting for transfers between devices: 462 us -> none  [per_device(): summed_one, summed_two = lax.psum((grad_one, grad_two), ('gx', 'gy'))]
    pallas_call x0 -> x1, Pallas kernels: none -> 50.3 us  [per_device(): pl.pallas_call(functools.partial(kernel, n_gx, n_gy, factor), out_shape=(...]
    ppermute x16 -> x0, starting transfers between devices: 49.7 us -> none  [the longest x8 29.2 us: padded_2(): lax.ppermute(tail, axis, [(i, (i + 1) % count) for i in range(ends)])]
    dot_general x54 -> x0, matrix products: 48.2 us -> none  [the longest x36 36.5 us: convolve(): jnp.einsum('ixyz,io->oxyz', window, kernel, preferred_element_type=jnp.fl...]
    another operation x18 -> x0, local copies, waits for them, and re-layouts: 6.96 us -> none  [convolve(): kernel = weight[shift_x, shift_y].reshape(3 * channels, channels)]
    concatenate x8 -> x0, other arithmetic: 6.32 us -> none  [the longest x4 4.2 us: depth_stack(): jnp.concatenate([padded[:, :, :, offset:offset + depth] for offset in ran...]
    unnamed x62 -> x14, local copies, waits for them, and re-layouts: 0.99 us -> 7.25 us
  transfers between devices with their start and end apart: 17 -> 0, of which waited for: 1 -> 0; matrix products, arithmetic and copies ran while one was open for 7% -> 0% of each run, Pallas kernels for 0% -> 0%
where the time goes in v1:
time: 58.4 us; the launch traced here: 58.2 us
  Pallas kernels  50.3 us (86%)
  local copies, waits for them, and re-layouts  7.25 us (12%)
  between operations  0.65 us (1%)
    pallas_call x1, Pallas kernels, per_device(): pl.pallas_call(functools.partial(kernel, n_gx, n_gy, factor), out_shape=(...  50.3 us
    unnamed x14, local copies, waits for them, and re-layouts  7.25 us

profile of v1, /device:TPU:1, one launch (start us, length us, event | category | flops | bytes accessed | tf_op | source)
XLA Modules:
  0.0 58.2 jit_solution(18008953519920059312)
XLA Ops:
  0.6 0.0 copy-start.4
  0.6 0.6 %copy-done.4 = s32[1,1,6]{2,1,0:T(1,128)S(1)} copy-done((s32[1,1,6]{2,1,0:T(1,128)S(1)}, s32[1,1,6]{2,1,0:T(1,128)}, u32[]{:S(2)}) %copy-start.4) | copy-done | bytes 48
  1.3 0.0 copy-start
  1.3 0.9 %copy-done = bf16[3,3,3,32,32]{4,3,2,1,0:T(8,128)(2,1)S(1)} copy-done((bf16[3,3,3,32,32]{4,3,2,1,0:T(8,128)(2,1)S(1)}, bf16[3,3,3,32,32]{4,3,2,1,0:T(8,128)(2,1)}, u32[]{:S(2)}) %copy-start) | copy-done | bytes 55320
  2.2 0.0 copy-start.1
  2.2 0.9 %copy-done.1 = bf16[3,3,3,32,32]{4,3,2,1,0:T(8,128)(2,1)S(1)} copy-done((bf16[3,3,3,32,32]{4,3,2,1,0:T(8,128)(2,1)S(1)}, bf16[3,3,3,32,32]{4,3,2,1,0:T(8,128)(2,1)}, u32[]{:S(2)}) %copy-start.1) | copy-done | bytes 55320
  3.2 0.0 copy-start.2
  3.2 0.9 %copy-done.2 = bf16[32,8,384]{2,1,0:T(8,128)(2,1)S(1)} copy-done((bf16[32,8,384]{2,1,0:T(8,128)(2,1)S(1)}, bf16[32,8,384]{2,1,0:T(8,128)(2,1)}, u32[]{:S(2)}) %copy-start.2) | copy-done | bytes 196632
  4.1 0.0 copy-start.3
  4.1 0.9 %copy-done.3 = bf16[32,8,384]{2,1,0:T(8,128)(2,1)S(1)} copy-done((bf16[32,8,384]{2,1,0:T(8,128)(2,1)S(1)}, bf16[32,8,384]{2,1,0:T(8,128)(2,1)}, u32[]{:S(2)}) %copy-start.3) | copy-done | bytes 196632
  5.0 50.3 %shard_map.84 = (bf16[256,384]{1,0:T(8,128)(2,1)S(1)}, bf16[256,384]{1,0:T(8,128)(2,1)S(1)}, f32[864,32]{1,0:T(8,128)S(1)}, f32[864,32]{1,0:T(8,128)S(1)}) custom-call(s32[1,1,6]{2,1,0:T(1,128)S(1)} %copy-done.4, bf16[256,384]{1,0:T(8,128)(2,1)S(1)} %bitcast.14, bf16[256,384]{1,0:T(8,128)(2,1)S(1)} %bitcast.15, bf16[864,32]{1,0:T(8,128)(2,1)S(1)} %bitcast.10, ...), custom_call_target="tpu_custom_call" | custom-call | tf_op jit(solution)/shard_map/pallas_call | solution.py:434
  55.3 0.7 %copy.13 = bf16[32,8,384]{2,1,0:T(8,128)(2,1)} copy(bf16[32,8,384]{2,1,0:T(8,128)(2,1)S(1)} %bitcast.13) | data formatting | bytes 393216
  56.0 0.7 %copy.14 = bf16[32,8,384]{2,1,0:T(8,128)(2,1)} copy(bf16[32,8,384]{2,1,0:T(8,128)(2,1)S(1)} %bitcast.12) | data formatting | bytes 393216
  56.7 0.8 %copy.15 = f32[3,3,3,32,32]{4,3,2,1,0:T(8,128)} copy(f32[3,3,3,32,32]{4,3,2,1,0:T(8,128)S(1)} %bitcast.9) | data formatting | bytes 221184
  57.4 0.8 %copy.16 = f32[3,3,3,32,32]{4,3,2,1,0:T(8,128)} copy(f32[3,3,3,32,32]{4,3,2,1,0:T(8,128)S(1)} %bitcast.8) | data formatting | bytes 221184
Async XLA Ops:
  0.6 0.7 %copy-start.4 = (s32[1,1,6]{2,1,0:T(1,128)S(1)}, s32[1,1,6]{2,1,0:T(1,128)}, u32[]{:S(2)}) copy-start(s32[1,1,6]{2,1,0:T(1,128)} %list_ref.1) | copy-start | bytes 76
  1.3 0.9 %copy-start = (bf16[3,3,3,32,32]{4,3,2,1,0:T(8,128)(2,1)S(1)}, bf16[3,3,3,32,32]{4,3,2,1,0:T(8,128)(2,1)}, u32[]{:S(2)}) copy-start(bf16[3,3,3,32,32]{4,3,2,1,0:T(8,128)(2,1)} %param.7) | copy-start | bytes 165892
  2.2 0.9 %copy-start.1 = (bf16[3,3,3,32,32]{4,3,2,1,0:T(8,128)(2,1)S(1)}, bf16[3,3,3,32,32]{4,3,2,1,0:T(8,128)(2,1)}, u32[]{:S(2)}) copy-start(bf16[3,3,3,32,32]{4,3,2,1,0:T(8,128)(2,1)} %param.8) | copy-start | bytes 165892
  3.2 0.9 %copy-start.2 = (bf16[32,8,384]{2,1,0:T(8,128)(2,1)S(1)}, bf16[32,8,384]{2,1,0:T(8,128)(2,1)}, u32[]{:S(2)}) copy-start(bf16[32,8,384]{2,1,0:T(8,128)(2,1)} %param.5) | copy-start | bytes 589828
  4.1 0.9 %copy-start.3 = (bf16[32,8,384]{2,1,0:T(8,128)(2,1)S(1)}, bf16[32,8,384]{2,1,0:T(8,128)(2,1)}, u32[]{:S(2)}) copy-start(bf16[32,8,384]{2,1,0:T(8,128)(2,1)} %param.9) | copy-start | bytes 589828

commit v2 on v1

--- a/solution.py
+++ b/solution.py
@@ -50,7 +50,7 @@
     lane = lax.broadcasted_iota(jnp.int32, (C, 128), 1)
     row = lax.broadcasted_iota(jnp.int32, (C, 128), 0)
     repeat = jnp.where(lane % C == row, 1.0, 0.0).astype(BF16)
-    quad[which] = dot(w_ref[...], repeat).astype(BF16).reshape(27, C, 128)
+    quad[which] = dot(w_ref[which], repeat).astype(BF16).reshape(27, C, 128)
 
 
 def build_bands(quad, band, rim_in, rim_out):
@@ -171,12 +171,14 @@
 
 def kernel(
     n_gx, n_gy, factor,
-    list_ref, f_ref, g_ref, w1_ref, w2_ref,
+    list_any, f_any, g_any, w1_any, w2_any,
     block_ref, back_ref, one_ref, two_ref,
     turned_a, cells_a, side_a, corner_a, rim_a,
     turned_b, cells_b, side_b, corner_b, rim_b,
     quad, band, rim_in, rim_out,
     packed, gathered, column, total,
+    list_ref, fields_in, weights_in,
+    list_sem, f_sem, g_sem, w1_sem, w2_sem,
     halo_send_a, halo_recv_a, halo_send_b, halo_recv_b,
     part_send, part_recv, line_send, line_recv, full_send, full_recv,
 ):
@@ -196,6 +198,19 @@
     def in_line(other):
         return (x_hi * n_line + other, gy)
 
+    loads = [
+        pltpu.make_async_copy(src, dst, sem)
+        for src, dst, sem in (
+            (list_any, list_ref, list_sem),
+            (f_any, fields_in.at[0], f_sem),
+            (g_any, fields_in.at[1], g_sem),
+            (w1_any, weights_in.at[0], w1_sem),
+            (w2_any, weights_in.at[1], w2_sem),
+        )
+    ]
+    for load in loads:
+        load.start()
+
     barrier = pltpu.get_barrier_semaphore()
     around = [(dx, dy) for dx in (-1, 0, 1) for dy in (-1, 0, 1) if (dx, dy) != (0, 0)]
     for dx, dy in around:
@@ -214,6 +229,7 @@
     lax.fori_loop(1, n_plane, greet_plane, 0)
     lax.fori_loop(1, n_line, greet_line, 0)
 
+    loads[0].wait()
     hits = []
     for brick in range(BRICKS):
         count = jnp.int32(0)
@@ -233,8 +249,9 @@
     col = lax.broadcasted_iota(jnp.int32, (LANES, LANES), 1)
     order = jnp.where(col == (row % C) * SIDE + row // C, 1.0, 0.0).astype(BF16)
     reorder = jnp.where(row == (col % C) * SIDE + col // C, 1.0, 0.0).astype(BF16)
-    for field, ref in enumerate((f_ref, g_ref)):
-        value = (dot(order, ref[...]) * across).astype(BF16)
+    for field in range(2):
+        loads[1 + field].wait()
+        value = (dot(order, fields_in[field]) * across).astype(BF16)
         turned_a[field] = value
         cells_a[field, pl.ds(NZ, OWN), :] = value.T
 
@@ -251,37 +268,44 @@
             return cells.at[:, pl.ds((y + 1) * NZ, NZ), :]
 
         plan = [
+            (strip(high, tail), corner.at[0], (1, 1)),
+            (strip(low, tail), corner.at[1], (-1, 1)),
+            (strip(high, head), corner.at[2], (1, -1)),
+            (strip(low, head), corner.at[3], (-1, -1)),
             (slab(SIDE - 1), slab(-1), (0, 1)),
             (slab(0), slab(SIDE), (0, -1)),
             (strip(high, every), side.at[0], (1, 0)),
             (strip(low, every), side.at[1], (-1, 0)),
-            (strip(high, tail), corner.at[0], (1, 1)),
-            (strip(low, tail), corner.at[1], (-1, 1)),
-            (strip(high, head), corner.at[2], (1, -1)),
-            (strip(low, head), corner.at[3], (-1, -1)),
         ]
         copies = []
-        for n, (src, dst, (dx, dy)) in enumerate(plan):
+        for src, dst, (dx, dy) in plan:
             copies.append(
                 pltpu.make_async_remote_copy(
                     src_ref=src,
                     dst_ref=dst,
-                    send_sem=send.at[n],
-                    recv_sem=recv.at[n],
+                    send_sem=send,
+                    recv_sem=recv,
                     device_id=beside(dx, dy),
                     device_id_type=MESH,
                 )
             )
         for copy in copies:
             copy.start()
-        return copies
+        whole = turned.at[:, :, pl.ds(0, 256)]
+        return pltpu.make_async_remote_copy(
+            src_ref=whole,
+            dst_ref=whole,
+            send_sem=send,
+            recv_sem=recv,
+            device_id=beside(1, 0),
+            device_id_type=MESH,
+        )
 
     def edge(condition):
         return jnp.where(condition, 1.0, 0.0).astype(F32)
 
     def place_rims(copies, cells, side, corner, rim):
-        for copy in copies:
-            copy.wait_recv()
+        copies.wait_recv()
         first_y, last_y = edge(gy > 0), edge(gy < n_gy - 1)
         first_x, last_x = edge(gx > 0), edge(gx < n_gx - 1)
         for rows, keep in ((pl.ds(0, NZ), first_y), (pl.ds(ALL - NZ, NZ), last_y)):
@@ -301,8 +325,9 @@
         rim[pl.ds(ALL - NZ, NZ), :] = lower.astype(BF16)
 
     copies_a = exchange(turned_a, cells_a, side_a, corner_a, halo_send_a, halo_recv_a)
-    widen_weights(w1_ref, quad, 0)
-    widen_weights(w2_ref, quad, 1)
+    for w in range(2):
+        loads[3 + w].wait()
+        widen_weights(weights_in, quad, w)
     build_bands(quad, band, rim_in, rim_out)
     place_rims(copies_a, cells_a, side_a, corner_a, rim_a)
 
@@ -329,59 +354,49 @@
     def share_of(ref, other):
         return ref.at[pl.ds(pl.multiple_of(other * share, share), share), :]
 
-    def part_copy(target, source):
+    def remote(src, dst, send, recv, device):
         return pltpu.make_async_remote_copy(
-            src_ref=share_of(packed, target),
-            dst_ref=gathered.at[source],
-            send_sem=part_send.at[target],
-            recv_sem=part_recv.at[source],
-            device_id=in_plane(target),
+            src_ref=src,
+            dst_ref=dst,
+            send_sem=send,
+            recv_sem=recv,
+            device_id=device,
             device_id_type=MESH,
         )
 
-    def line_copy(target, source):
-        return pltpu.make_async_remote_copy(
-            src_ref=column.at[line],
-            dst_ref=column.at[source],
-            send_sem=line_send.at[target],
-            recv_sem=line_recv.at[source],
-            device_id=in_line(target),
-            device_id_type=MESH,
-        )
-
-    def full_copy(target, source):
-        return pltpu.make_async_remote_copy(
-            src_ref=share_of(total, rank),
-            dst_ref=share_of(total, source),
-            send_sem=full_send.at[target],
-            recv_sem=full_recv.at[source],
-            device_id=in_plane(target),
-            device_id_type=MESH,
-        )
-
-    def each(make, me, count, act):
+    def part_copy(target):
+        src, dst = share_of(packed, target), gathered.at[rank]
+        return remote(src, dst, part_send, part_recv, in_plane(target))
+
+    def line_copy(target):
+        src, dst = column.at[line], column.at[line]
+        return remote(src, dst, line_send, line_recv, in_line(target))
+
+    def full_copy(target):
+        src, dst = share_of(total, rank), share_of(total, rank)
+        return remote(src, dst, full_send, full_recv, in_plane(target))
+
+    def start_all(make, me, count):
         def step(d, carry):
-            act(make, me, lax.rem(me + d, count))
+            make(lax.rem(me + d, count)).start()
             return carry
 
         lax.fori_loop(1, count, step, 0)
 
-    def start(make, me, other):
-        make(other, me).start()
-
-    def landed(make, me, other):
-        make(other, other).wait_recv()
-
-    def sent(make, me, other):
-        make(other, me).wait_send()
+    most = gathered.at[pl.ds(0, n_plane - 1)]
+    part_all = remote(most, most, part_send, part_recv, beside(1, 0))
+    most = column.at[pl.ds(0, n_line - 1)]
+    line_all = remote(most, most, line_send, line_recv, beside(1, 0))
+    most = total.at[pl.ds(0, (n_plane - 1) * share)]
+    full_all = remote(most, most, full_send, full_recv, beside(1, 0))
 
     def summed(ref, count):
-        value = ref[0]
+        value = ref[0].astype(F32)
         for n in range(1, count):
-            value = value + ref[n]
+            value = value + ref[n].astype(F32)
         return value
 
-    each(part_copy, rank, n_plane, start)
+    start_all(part_copy, rank, n_plane)
     gathered[rank] = packed[pl.ds(pl.multiple_of(rank * share, share), share), :]
 
     place_rims(copies_b, cells_b, side_b, corner_b, rim_b)
@@ -390,22 +405,20 @@
     block_out = (cells_a[0, middle, :].astype(F32) + pre_two).astype(BF16)
     block_ref[...] = dot(reorder, block_out, ((1,), (1,))).astype(BF16)
 
-    each(part_copy, rank, n_plane, landed)
-    column[line] = summed(gathered, n_plane)
-    each(line_copy, line, n_line, start)
+    part_all.wait_recv()
+    column[line] = summed(gathered, n_plane).astype(BF16)
+    start_all(line_copy, line, n_line)
 
     back = conv_backward(cells_b, rim_b, band, rim_out, 0) * occupied
     grad_features = (cells_a[1, middle, :].astype(F32) + back).astype(BF16)
     back_ref[...] = dot(reorder, grad_features, ((1,), (1,))).astype(BF16)
 
-    each(line_copy, line, n_line, landed)
+    line_all.wait_recv()
     total[pl.ds(pl.multiple_of(rank * share, share), share), :] = summed(column, n_line)
-    each(full_copy, rank, n_plane, start)
-    for copy in copies_a + copies_b:
-        copy.wait_send()
-    each(part_copy, rank, n_plane, sent)
-    each(line_copy, line, n_line, sent)
-    each(full_copy, rank, n_plane, landed)
+    start_all(full_copy, rank, n_plane)
+    for copies in (copies_a, copies_b, part_all, line_all):
+        copies.wait_send()
+    full_all.wait_recv()
 
     for n, first in enumerate(range(0, 27, 4)):
         count = min(4, 27 - first)
@@ -415,7 +428,16 @@
         group = total[pl.ds((7 + n) * C, C), :] * factor
         for k in range(count):
             two_ref[pl.ds((first + k) * C, C), :] = group[:, k * C : (k + 1) * C]
-    each(full_copy, rank, n_plane, sent)
+    full_all.wait_send()
+
+
+def deliver(*refs):
+    results, outs, sems = refs[:4], refs[4:8], refs[8:]
+    copies = [pltpu.make_async_copy(*part) for part in zip(results, outs, sems)]
+    for copy in copies:
+        copy.start()
+    for copy in copies:
+        copy.wait()
 
 
 def per_device(features, brick_list, weight_one, weight_two, cotangent):
@@ -431,15 +453,23 @@
         pltpu.VMEM((4, 2, C, 128), BF16),
         pltpu.VMEM((ALL, 128), BF16),
     ]
-    block_out, grad_features, one, two = pl.pallas_call(
+    out_shape = (
+        jax.ShapeDtypeStruct((LANES, OWN), BF16),
+        jax.ShapeDtypeStruct((LANES, OWN), BF16),
+        jax.ShapeDtypeStruct((27 * C, C), F32),
+        jax.ShapeDtypeStruct((27 * C, C), F32),
+    )
+    arguments = (
+        brick_list,
+        features.reshape(LANES, OWN),
+        cotangent.reshape(LANES, OWN),
+        weight_one.reshape(27 * C, C),
+        weight_two.reshape(27 * C, C),
+    )
+    results = pl.pallas_call(
         functools.partial(kernel, n_gx, n_gy, factor),
-        out_shape=(
-            jax.ShapeDtypeStruct((LANES, OWN), BF16),
-            jax.ShapeDtypeStruct((LANES, OWN), BF16),
-            jax.ShapeDtypeStruct((27 * C, C), F32),
-            jax.ShapeDtypeStruct((27 * C, C), F32),
-        ),
-        in_specs=[pl.BlockSpec(memory_space=pltpu.SMEM)] + [vmem] * 4,
+        out_shape=tuple(pltpu.VMEM(result.shape, result.dtype) for result in out_shape),
+        in_specs=[pl.BlockSpec(memory_space=pltpu.HBM)] * 5,
         out_specs=[vmem] * 4,
         scratch_shapes=halo
         + halo
@@ -450,23 +480,26 @@
             pltpu.VMEM((2, 3, LANES, 3 * 128), BF16),
             pltpu.VMEM((PACKED, 128), F32),
             pltpu.VMEM((n_plane, share, 128), F32),
-            pltpu.VMEM((n_line, share, 128), F32),
+            pltpu.VMEM((n_line, share, 128), BF16),
             pltpu.VMEM((PACKED, 128), F32),
         ]
-        + [pltpu.SemaphoreType.DMA((8,))] * 4
-        + [pltpu.SemaphoreType.DMA((n_plane,))] * 2
-        + [pltpu.SemaphoreType.DMA((n_line,))] * 2
-        + [pltpu.SemaphoreType.DMA((n_plane,))] * 2,
+        + [
+            pltpu.SMEM((1, 1, BRICKS), jnp.int32),
+            pltpu.VMEM((2, LANES, OWN), BF16),
+            pltpu.VMEM((2, 27 * C, C), BF16),
+        ]
+        + [pltpu.SemaphoreType.DMA] * 15,
         compiler_params=pltpu.CompilerParams(
-            collective_id=0, has_side_effects=True, vmem_limit_bytes=48 * 1024 * 1024
+            collective_id=0, has_side_effects=True, vmem_limit_bytes=40 * 1024 * 1024
         ),
-    )(
-        brick_list,
-        features.reshape(LANES, OWN),
-        cotangent.reshape(LANES, OWN),
-        weight_one.reshape(27 * C, C),
-        weight_two.reshape(27 * C, C),
-    )
+    )(*[pltpu.with_memory_space_constraint(value, pltpu.HBM) for value in arguments])
+    block_out, grad_features, one, two = pl.pallas_call(
+        deliver,
+        out_shape=out_shape,
+        in_specs=[vmem] * 4,
+        out_specs=[pl.BlockSpec(memory_space=pl.ANY)] * 4,
+        scratch_shapes=[pltpu.SemaphoreType.DMA] * 4,
+    )(*results)
     flat = (C, SIDE, OWN)
     cube = (3, 3, 3, C, C)
     return block_out.reshape(flat), grad_features.reshape(flat), one.reshape(cube), two.reshape(cube)

time: 58.4 us -> 51.4 us (0.88)
  local copies, waits for them, and re-layouts: 7.25 us -> 2.87 us
  Pallas kernels: 50.3 us -> 47.8 us
    unnamed x14 -> x8, local copies, waits for them, and re-layouts: 7.25 us -> 2.87 us
    pallas_call x1 -> x2, Pallas kernels: 50.3 us -> 47.8 us  [the longest x1 45.3 us: per_device(): pl.pallas_call(functools.partial(kernel, n_gx, n_gy, factor), out_shape=t...]
where the time goes in v2:
time: 51.4 us; the launch traced here: 51.3 us
  Pallas kernels  47.8 us (93%)
  local copies, waits for them, and re-layouts  2.87 us (6%)
  between operations  0.65 us (1%)
    pallas_call x1, Pallas kernels, per_device(): pl.pallas_call(functools.partial(kernel, n_gx, n_gy, factor), out_shape=t...  45.3 us
    unnamed x8, local copies, waits for them, and re-layouts  2.87 us
    pallas_call x1, Pallas kernels, per_device(): pl.pallas_call(deliver, out_shape=out_shape, in_specs=[vmem] * 4, out_spe...  2.42 us

profile of v2, /device:TPU:1, one launch (start us, length us, event | category | flops | bytes accessed | tf_op | source)
XLA Modules:
  0.0 51.3 jit_solution(819143183409914261)
XLA Ops:
  0.6 45.3 %shard_map.84 = (bf16[256,384]{1,0:T(8,128)(2,1)S(1)}, bf16[256,384]{1,0:T(8,128)(2,1)S(1)}, f32[864,32]{1,0:T(8,128)S(1)}, f32[864,32]{1,0:T(8,128)S(1)}) custom-call(s32[1,1,6]{2,1,0:T(1,128)} %list_any.1, bf16[256,384]{1,0:T(8,128)(2,1)} %bitcast.10, bf16[256,384]{1,0:T(8,128)(2,1)} %bitcast.11, bf16[864,32]{1,0:T(8,128)(2,1)} %bitcast.8, ...), custom_call_target="tpu_custom_call" | custom-call | tf_op jit(solution)/shard_map/pallas_call | solution.py:469
  46.0 0.0 copy-start
  46.0 0.8 %copy-done = f32[864,32]{1,0:T(8,128)} copy-done((f32[864,32]{1,0:T(8,128)}, f32[864,32]{1,0:T(8,128)S(1)}, u32[]{:S(2)}) %copy-start) | copy-done | bytes 110616
  46.7 0.0 copy-start.1
  46.8 0.8 %copy-done.1 = f32[864,32]{1,0:T(8,128)} copy-done((f32[864,32]{1,0:T(8,128)}, f32[864,32]{1,0:T(8,128)S(1)}, u32[]{:S(2)}) %copy-start.1) | copy-done | bytes 110616
  47.5 0.0 copy-start.2
  47.5 0.7 %copy-done.2 = bf16[256,384]{1,0:T(8,128)(2,1)} copy-done((bf16[256,384]{1,0:T(8,128)(2,1)}, bf16[256,384]{1,0:T(8,128)(2,1)S(1)}, u32[]{:S(2)}) %copy-start.2) | copy-done | bytes 196632
  48.2 0.0 copy-start.3
  48.2 0.7 %copy-done.3 = bf16[256,384]{1,0:T(8,128)(2,1)} copy-done((bf16[256,384]{1,0:T(8,128)(2,1)}, bf16[256,384]{1,0:T(8,128)(2,1)S(1)}, u32[]{:S(2)}) %copy-start.3) | copy-done | bytes 196632
  48.9 2.4 %shard_map.85 = (bf16[256,384]{1,0:T(8,128)(2,1)}, bf16[256,384]{1,0:T(8,128)(2,1)}, f32[864,32]{1,0:T(8,128)}, f32[864,32]{1,0:T(8,128)}) custom-call(bf16[256,384]{1,0:T(8,128)(2,1)} %copy-done.2, bf16[256,384]{1,0:T(8,128)(2,1)} %copy-done.3, f32[864,32]{1,0:T(8,128)} %copy-done, f32[864,32]{1,0:T(8,128)} %copy-done.1), custom_call_target="tpu_custom_call" | custom-call | tf_op jit(solution)/shard_map/pallas_call | solution.py:496
Async XLA Ops:
  46.0 0.8 %copy-start = (f32[864,32]{1,0:T(8,128)}, f32[864,32]{1,0:T(8,128)S(1)}, u32[]{:S(2)}) copy-start(f32[864,32]{1,0:T(8,128)S(1)} %get-tuple-element.14.refs_2_) | copy-start | bytes 331780
  46.7 0.8 %copy-start.1 = (f32[864,32]{1,0:T(8,128)}, f32[864,32]{1,0:T(8,128)S(1)}, u32[]{:S(2)}) copy-start(f32[864,32]{1,0:T(8,128)S(1)} %get-tuple-element.15.refs_3_) | copy-start | bytes 331780
  47.5 0.7 %copy-start.2 = (bf16[256,384]{1,0:T(8,128)(2,1)}, bf16[256,384]{1,0:T(8,128)(2,1)S(1)}, u32[]{:S(2)}) copy-start(bf16[256,384]{1,0:T(8,128)(2,1)S(1)} %get-tuple-element.12.refs_0_) | copy-start | bytes 589828
  48.2 0.7 %copy-start.3 = (bf16[256,384]{1,0:T(8,128)(2,1)}, bf16[256,384]{1,0:T(8,128)(2,1)S(1)}, u32[]{:S(2)}) copy-start(bf16[256,384]{1,0:T(8,128)(2,1)S(1)} %get-tuple-element.13.refs_1_) | copy-start | bytes 589828

commit v3 on v2

--- a/solution.py
+++ b/solution.py
@@ -185,19 +185,46 @@
     gx, gy = lax.axis_index("gx"), lax.axis_index("gy")
     n_line = n_gx // X_HI
     n_plane = X_HI * n_gy
-    x_hi, line = gx // n_line, lax.rem(gx, n_line)
+    x_hi = jnp.where(gx >= n_line, 1, 0)
+    line = gx - x_hi * n_line
     rank = x_hi * n_gy + gy
     share = PACKED // n_plane
+    n_seats = n_plane // 2
+    n_busy = -(-7 * C // share)
+    seat = rank // 2
+    half = rank - 2 * seat
+    busy = seat < n_busy
+
+    def wrapped(value, count):
+        value = jnp.where(value >= count, value - count, value)
+        return jnp.where(value < 0, value + count, value)
 
     def beside(dx, dy):
-        return (lax.rem(gx + dx + n_gx, n_gx), lax.rem(gy + dy + n_gy, n_gy))
+        return (wrapped(gx + dx, n_gx), wrapped(gy + dy, n_gy))
 
     def in_plane(other):
-        return (other // n_gy * n_line + line, lax.rem(other, n_gy))
+        hi = jnp.where(other >= n_gy, 1, 0)
+        return (hi * n_line + line, other - hi * n_gy)
 
     def in_line(other):
         return (x_hi * n_line + other, gy)
 
+    barrier = pltpu.get_barrier_semaphore()
+    around = [(dx, dy) for dx in (-1, 0, 1) for dy in (-1, 0, 1) if (dx, dy) != (0, 0)]
+    def greet_plane(d, carry):
+        target = in_plane(wrapped(rank + d, n_plane))
+        pl.semaphore_signal(barrier, inc=1, device_id=target, device_id_type=MESH)
+        return carry
+
+    def greet_line(d, carry):
+        target = in_line(wrapped(line + d, n_line))
+        pl.semaphore_signal(barrier, inc=1, device_id=target, device_id_type=MESH)
+        return carry
+
+    lax.fori_loop(1, n_line, greet_line, 0)
+    lax.fori_loop(1, n_plane, greet_plane, 0)
+    for dx, dy in around:
+        pl.semaphore_signal(barrier, inc=1, device_id=beside(dx, dy), device_id_type=MESH)
     loads = [
         pltpu.make_async_copy(src, dst, sem)
         for src, dst, sem in (
@@ -210,24 +237,6 @@
     ]
     for load in loads:
         load.start()
-
-    barrier = pltpu.get_barrier_semaphore()
-    around = [(dx, dy) for dx in (-1, 0, 1) for dy in (-1, 0, 1) if (dx, dy) != (0, 0)]
-    for dx, dy in around:
-        pl.semaphore_signal(barrier, inc=1, device_id=beside(dx, dy), device_id_type=MESH)
-
-    def greet_plane(d, carry):
-        target = in_plane(lax.rem(rank + d, n_plane))
-        pl.semaphore_signal(barrier, inc=1, device_id=target, device_id_type=MESH)
-        return carry
-
-    def greet_line(d, carry):
-        target = in_line(lax.rem(line + d, n_line))
-        pl.semaphore_signal(barrier, inc=1, device_id=target, device_id_type=MESH)
-        return carry
-
-    lax.fori_loop(1, n_plane, greet_plane, 0)
-    lax.fori_loop(1, n_line, greet_line, 0)
 
     loads[0].wait()
     hits = []
@@ -267,62 +276,76 @@
         def slab(y):
             return cells.at[:, pl.ds((y + 1) * NZ, NZ), :]
 
-        plan = [
-            (strip(high, tail), corner.at[0], (1, 1)),
-            (strip(low, tail), corner.at[1], (-1, 1)),
-            (strip(high, head), corner.at[2], (1, -1)),
-            (strip(low, head), corner.at[3], (-1, -1)),
-            (slab(SIDE - 1), slab(-1), (0, 1)),
-            (slab(0), slab(SIDE), (0, -1)),
-            (strip(high, every), side.at[0], (1, 0)),
-            (strip(low, every), side.at[1], (-1, 0)),
-        ]
-        copies = []
-        for src, dst, (dx, dy) in plan:
-            copies.append(
-                pltpu.make_async_remote_copy(
-                    src_ref=src,
-                    dst_ref=dst,
-                    send_sem=send,
-                    recv_sem=recv,
-                    device_id=beside(dx, dy),
-                    device_id_type=MESH,
-                )
+        def remote_copy(src, dst, group, dx, dy):
+            return pltpu.make_async_remote_copy(
+                src_ref=src,
+                dst_ref=dst,
+                send_sem=send.at[group],
+                recv_sem=recv.at[group],
+                device_id=beside(dx, dy),
+                device_id_type=MESH,
             )
-        for copy in copies:
-            copy.start()
-        whole = turned.at[:, :, pl.ds(0, 256)]
-        return pltpu.make_async_remote_copy(
-            src_ref=whole,
-            dst_ref=whole,
-            send_sem=send,
-            recv_sem=recv,
-            device_id=beside(1, 0),
-            device_id_type=MESH,
-        )
-
-    def edge(condition):
-        return jnp.where(condition, 1.0, 0.0).astype(F32)
+
+        @pl.when(gx < n_gx - 1)
+        def _():
+            remote_copy(strip(high, tail), corner.at[0], 1, 1, 1).start()
+            remote_copy(strip(high, head), corner.at[2], 1, 1, -1).start()
+            remote_copy(strip(high, every), side.at[0], 1, 1, 0).start()
+
+        @pl.when(gx > 0)
+        def _():
+            remote_copy(strip(low, tail), corner.at[1], 2, -1, 1).start()
+            remote_copy(strip(low, head), corner.at[3], 2, -1, -1).start()
+            remote_copy(strip(low, every), side.at[1], 2, -1, 0).start()
+
+        remote_copy(slab(SIDE - 1), slab(-1), 0, 0, 1).start()
+        remote_copy(slab(0), slab(SIDE), 0, 0, -1).start()
+
+        slabs = turned.at[0, pl.ds(0, 2 * NZ * 2), pl.ds(0, 256)]
+        strips = turned.at[0, pl.ds(0, 160), pl.ds(0, 256)]
+
+        def wait_recv():
+            remote_copy(slabs, slabs, 0, 0, 1).wait_recv()
+
+            @pl.when(gx > 0)
+            def _():
+                remote_copy(strips, strips, 1, 1, 0).wait_recv()
+
+            @pl.when(gx < n_gx - 1)
+            def _():
+                remote_copy(strips, strips, 2, 1, 0).wait_recv()
+
+        def wait_send():
+            remote_copy(slabs, slabs, 0, 0, 1).wait_send()
+
+            @pl.when(gx < n_gx - 1)
+            def _():
+                remote_copy(strips, strips, 1, 1, 0).wait_send()
+
+            @pl.when(gx > 0)
+            def _():
+                remote_copy(strips, strips, 2, 1, 0).wait_send()
+
+        return wait_recv, wait_send
 
     def place_rims(copies, cells, side, corner, rim):
-        copies.wait_recv()
-        first_y, last_y = edge(gy > 0), edge(gy < n_gy - 1)
-        first_x, last_x = edge(gx > 0), edge(gx < n_gx - 1)
+        copies[0]()
+        first_y, last_y = gy > 0, gy < n_gy - 1
         for rows, keep in ((pl.ds(0, NZ), first_y), (pl.ds(ALL - NZ, NZ), last_y)):
             for field in range(2):
-                cells[field, rows, :] = (cells[field, rows, :].astype(F32) * keep).astype(BF16)
-        odd = lax.rem(lane_block((1, 128)), 2) == 1
-        keep_x = jnp.where(odd, last_x, first_x)
-
-        def turn(left, right):
+                kept = jnp.where(keep, cells[field, rows, :].astype(F32), 0.0)
+                cells[field, rows, :] = kept.astype(BF16)
+        odd = lax.rem(lane_block((1, 128)), 2)
+        inside = jnp.where(odd == 1, jnp.where(gx < n_gx - 1, 1, 0), jnp.where(gx > 0, 1, 0))
+
+        def turn(left, right, keep):
             parts = [left[0], right[0], left[1], right[1]]
-            return jnp.concatenate(parts, axis=0).T.astype(F32) * keep_x
-
-        rim[pl.ds(NZ, OWN), :] = turn(side[0], side[1]).astype(BF16)
-        upper = turn(corner[0], corner[1])[128 - NZ :] * first_y
-        lower = turn(corner[2], corner[3])[:NZ] * last_y
-        rim[pl.ds(0, NZ), :] = upper.astype(BF16)
-        rim[pl.ds(ALL - NZ, NZ), :] = lower.astype(BF16)
+            value = jnp.concatenate(parts, axis=0).T.astype(F32)
+            return jnp.where(inside * jnp.where(keep, 1, 0) > 0, value, 0.0).astype(BF16)
+
+        rim[pl.ds(NZ, OWN), :] = turn(side[0], side[1], True)
+        rim[pl.ds(0, NZ), :] = turn(corner[0], corner[1], first_y)[128 - NZ :]
+        rim[pl.ds(ALL - NZ, NZ), :] = turn(corner[2], corner[3], last_y)[:NZ]
 
     copies_a = exchange(turned_a, cells_a, side_a, corner_a, halo_send_a, halo_recv_a)
     for w in range(2):
@@ -339,20 +362,11 @@
     for field, value in enumerate((hidden, delta)):
         cells_b[field, pl.ds(NZ, OWN), :] = value
         turned_b[field] = value.T
-    copies_b = exchange(turned_b, cells_b, side_b, corner_b, halo_send_b, halo_recv_b)
-
-    sums_two = kernel_sums(hidden, cells_a, rim_a, 1)
-    sums_one = kernel_sums(delta, cells_a, rim_a, 0)
-    offsets = [(kx, ky, kz) for kx in (-1, 0, 1) for ky in (-1, 0, 1) for kz in (-1, 0, 1)]
-    one = [sums_one[k] for k in offsets] + [jnp.zeros((C, 128), F32)]
-    two = [sums_two[-k[0], -k[1], -k[2]] for k in offsets] + [jnp.zeros((C, 128), F32)]
-    for n, start in enumerate(range(0, 28, 4)):
-        packed[pl.ds(n * C, C), :] = fold_four(*one[start : start + 4])
-        packed[pl.ds((7 + n) * C, C), :] = fold_four(*two[start : start + 4])
-    packed[pl.ds(14 * C, PACKED - 14 * C), :] = jnp.zeros((PACKED - 14 * C, 128), F32)
 
     def share_of(ref, other):
-        return ref.at[pl.ds(pl.multiple_of(other * share, share), share), :]
+        other_seat = other // 2
+        top = (other - 2 * other_seat) * (PACKED // 2) + other_seat * share
+        return ref.at[pl.ds(pl.multiple_of(top, share), share), :]
 
     def remote(src, dst, send, recv, device):
         return pltpu.make_async_remote_copy(
@@ -376,19 +390,58 @@
         src, dst = share_of(total, rank), share_of(total, rank)
         return remote(src, dst, full_send, full_recv, in_plane(target))
 
+    def start_parts(which):
+        def step(d, carry):
+            other = wrapped(seat + d, n_seats)
+
+            @pl.when((other < n_busy) & (2 * other + which != rank))
+            def _():
+                part_copy(2 * other + which).start()
+
+            return carry
+
+        lax.fori_loop(0, n_seats, step, 0)
+
     def start_all(make, me, count):
         def step(d, carry):
-            make(lax.rem(me + d, count)).start()
+            make(wrapped(me + d, count)).start()
             return carry
 
         lax.fori_loop(1, count, step, 0)
 
-    most = gathered.at[pl.ds(0, n_plane - 1)]
-    part_all = remote(most, most, part_send, part_recv, beside(1, 0))
-    most = column.at[pl.ds(0, n_line - 1)]
-    line_all = remote(most, most, line_send, line_recv, beside(1, 0))
-    most = total.at[pl.ds(0, (n_plane - 1) * share)]
-    full_all = remote(most, most, full_send, full_recv, beside(1, 0))
+    def whole(ref, count, send, recv):
+        part = ref.at[pl.ds(0, count)]
+        return remote(part, part, send, recv, beside(1, 0))
+
+    part_all = whole(gathered, n_plane - 1, part_send, part_recv)
+    line_all = whole(column, n_line - 1, line_send, line_recv)
+
+    def when_busy(busy_act, idle_act):
+        pl.when(busy)(busy_act)
+        if n_busy < n_seats:
+            pl.when(jnp.logical_not(busy))(idle_act)
+
+    def nothing():
+        pass
+
+    def wait_parts_sent():
+        sent = 2 * n_busy
+        when_busy(
+            whole(gathered, sent - 1, part_send, part_recv).wait_send,
+            whole(gathered, sent, part_send, part_recv).wait_send,
+        )
+
+    def wait_full():
+        landed = 2 * n_busy * share
+        when_busy(
+            whole(total, landed - share, full_send, full_recv).wait_recv,
+            whole(total, landed, full_send, full_recv).wait_recv,
+        )
+
+    def wait_full_sent():
+        when_busy(
+            whole(total, (n_plane - 1) * share, full_send, full_recv).wait_send, nothing
+        )
 
     def summed(ref, count):
         value = ref[0].astype(F32)
@@ -396,39 +449,56 @@
             value = value + ref[n].astype(F32)
         return value
 
-    start_all(part_copy, rank, n_plane)
-    gathered[rank] = packed[pl.ds(pl.multiple_of(rank * share, share), share), :]
+    offsets = [(kx, ky, kz) for kx in (-1, 0, 1) for ky in (-1, 0, 1) for kz in (-1, 0, 1)]
+    for which, own, field, sign in ((0, hidden, 1, -1), (1, delta, 0, 1)):
+        sums = kernel_sums(own, cells_a, rim_a, field)
+        parts = [sums[tuple(sign * o for o in offset)] for offset in offsets]
+        parts.append(jnp.zeros((C, 128), F32))
+        top = which * (PACKED // 2)
+        for n, first in enumerate(range(0, 28, 4)):
+            packed[pl.ds(top + n * C, C), :] = fold_four(*parts[first : first + 4])
+        packed[pl.ds(top + 7 * C, C), :] = jnp.zeros((C, 128), F32)
+        start_parts(which)
+
+    copies_b = exchange(turned_b, cells_b, side_b, corner_b, halo_send_b, halo_recv_b)
+
+    @pl.when(busy)
+    def _():
+        gathered[rank] = share_of(packed, rank)[...]
+        part_all.wait_recv()
+        column[line] = summed(gathered, n_plane).astype(BF16)
+        start_all(line_copy, line, n_line)
 
     place_rims(copies_b, cells_b, side_b, corner_b, rim_b)
     pre_two = conv_forward(cells_b, rim_b, band, rim_in, 1) * occupied
     middle = pl.ds(NZ, OWN)
     block_out = (cells_a[0, middle, :].astype(F32) + pre_two).astype(BF16)
     block_ref[...] = dot(reorder, block_out, ((1,), (1,))).astype(BF16)
-
-    part_all.wait_recv()
-    column[line] = summed(gathered, n_plane).astype(BF16)
-    start_all(line_copy, line, n_line)
-
     back = conv_backward(cells_b, rim_b, band, rim_out, 0) * occupied
     grad_features = (cells_a[1, middle, :].astype(F32) + back).astype(BF16)
     back_ref[...] = dot(reorder, grad_features, ((1,), (1,))).astype(BF16)
 
-    line_all.wait_recv()
-    total[pl.ds(pl.multiple_of(rank * share, share), share), :] = summed(column, n_line)
-    start_all(full_copy, rank, n_plane)
-    for copies in (copies_a, copies_b, part_all, line_all):
-        copies.wait_send()
-    full_all.wait_recv()
+    @pl.when(busy)
+    def _():
+        line_all.wait_recv()
+        share_of(total, rank)[...] = summed(column, n_line).astype(BF16)
+        start_all(full_copy, rank, n_plane)
+
+    copies_a[1]()
+    copies_b[1]()
+    wait_parts_sent()
+    pl.when(busy)(line_all.wait_send)
+    wait_full()
 
     for n, first in enumerate(range(0, 27, 4)):
         count = min(4, 27 - first)
         one_ref[pl.ds(first * C, count * C), :] = (
-            total[pl.ds(n * C, C), :].T[: count * C] * factor
-        )
-        group = total[pl.ds((7 + n) * C, C), :] * factor
+            total[pl.ds(PACKED // 2 + n * C, C), :].astype(F32).T[: count * C] * factor
+        )
+        group = total[pl.ds(n * C, C), :].astype(F32) * factor
         for k in range(count):
             two_ref[pl.ds((first + k) * C, C), :] = group[:, k * C : (k + 1) * C]
-    full_all.wait_send()
+    wait_full_sent()
 
 
 def deliver(*refs):
@@ -481,14 +551,16 @@
             pltpu.VMEM((PACKED, 128), F32),
             pltpu.VMEM((n_plane, share, 128), F32),
             pltpu.VMEM((n_line, share, 128), BF16),
-            pltpu.VMEM((PACKED, 128), F32),
+            pltpu.VMEM((PACKED, 128), BF16),
         ]
         + [
             pltpu.SMEM((1, 1, BRICKS), jnp.int32),
             pltpu.VMEM((2, LANES, OWN), BF16),
             pltpu.VMEM((2, 27 * C, C), BF16),
         ]
-        + [pltpu.SemaphoreType.DMA] * 15,
+        + [pltpu.SemaphoreType.DMA] * 5
+        + [pltpu.SemaphoreType.DMA((3,))] * 4
+        + [pltpu.SemaphoreType.DMA] * 6,
         compiler_params=pltpu.CompilerParams(
             collective_id=0, has_side_effects=True, vmem_limit_bytes=40 * 1024 * 1024
         ),
@@ -499,7 +571,8 @@
         in_specs=[vmem] * 4,
         out_specs=[pl.BlockSpec(memory_space=pl.ANY)] * 4,
         scratch_shapes=[pltpu.SemaphoreType.DMA] * 4,
-    )(*results)
+        compiler_params=pltpu.CompilerParams(vmem_limit_bytes=4 * 1024 * 1024),
+    )(*[pltpu.with_memory_space_constraint(value, pltpu.VMEM) for value in results])
     flat = (C, SIDE, OWN)
     cube = (3, 3, 3, C, C)
     return block_out.reshape(flat), grad_features.reshape(flat), one.reshape(cube), two.reshape(cube)

time: 51.4 us -> 45.1 us (0.88)
  Pallas kernels: 47.8 us -> 44.3 us
  local copies, waits for them, and re-layouts: 2.87 us -> 0 us
    unnamed x8 -> x0, local copies, waits for them, and re-layouts: 2.87 us -> none
    pallas_call x1, Pallas kernels: 45.3 us -> 43.3 us  [per_device(): pl.pallas_call(functools.partial(kernel, n_gx, n_gy, factor), out_shape=t...]
    pallas_call x1, Pallas kernels: 2.42 us -> 1.07 us  [per_device(): pl.pallas_call(deliver, out_shape=out_shape, in_specs=[vmem] * 4, out_spe...]
where the time goes in v3:
time: 45.1 us; the launch traced here: 45 us
  Pallas kernels  44.3 us (98%)
  between operations  0.64 us (1%)
    pallas_call x1, Pallas kernels, per_device(): pl.pallas_call(functools.partial(kernel, n_gx, n_gy, factor), out_shape=t...  43.3 us
    pallas_call x1, Pallas kernels, per_device(): pl.pallas_call(deliver, out_shape=out_shape, in_specs=[vmem] * 4, out_spe...  1.07 us

profile of v3, /device:TPU:1, one launch (start us, length us, event | category | flops | bytes accessed | tf_op | source)
XLA Modules:
  0.0 45.0 jit_solution(13956240689819692821)
XLA Ops:
  0.6 43.3 %shard_map.84 = (bf16[256,384]{1,0:T(8,128)(2,1)S(1)}, bf16[256,384]{1,0:T(8,128)(2,1)S(1)}, f32[864,32]{1,0:T(8,128)S(1)}, f32[864,32]{1,0:T(8,128)S(1)}) custom-call(s32[1,1,6]{2,1,0:T(1,128)} %list_any.1, bf16[256,384]{1,0:T(8,128)(2,1)} %bitcast.10, bf16[256,384]{1,0:T(8,128)(2,1)} %bitcast.11, bf16[864,32]{1,0:T(8,128)(2,1)} %bitcast.8, ...), custom_call_target="tpu_custom_call" | custom-call | tf_op jit(solution)/shard_map/pallas_call | solution.py:539
  43.9 1.1 %shard_map.85 = (bf16[256,384]{1,0:T(8,128)(2,1)}, bf16[256,384]{1,0:T(8,128)(2,1)}, f32[864,32]{1,0:T(8,128)}, f32[864,32]{1,0:T(8,128)}) custom-call(bf16[256,384]{1,0:T(8,128)(2,1)S(1)} %get-tuple-element.12.refs_0_, bf16[256,384]{1,0:T(8,128)(2,1)S(1)} %get-tuple-element.13.refs_1_, f32[864,32]{1,0:T(8,128)S(1)} %get-tuple-element.14.refs_2_, ...), custom_call_target="tpu_custom_call" | custom-call | tf_op jit(solution)/shard_map/pallas_call | solution.py:568

commit v4 on v3

--- a/solution.py
+++ b/solution.py
@@ -15,7 +15,10 @@
 OWN = SIDE * NZ
 ALL = OWN + 2 * NZ
 PACKED = 512
+PIECES = 4
 X_HI = 2
+X_LO = 2
+CORES = 2
 MESH = pl.DeviceIdType.MESH
 F32 = jnp.float32
 BF16 = jnp.bfloat16
@@ -209,20 +212,34 @@
     def in_line(other):
         return (x_hi * n_line + other, gy)
 
+    n_x, n_y = X_HI * X_LO, n_gy // (X_LO * CORES)
+    y = gy // (X_LO * CORES)
+    x = x_hi * X_LO + gy // CORES - y * X_LO
+
+    def hops(offset, count):
+        return min(offset, count - offset)
+
+    chips = [(dy, dx) for dy in range(n_y) for dx in range(n_x)]
+    chips.sort(key=lambda chip: -hops(chip[0], n_y) - hops(chip[1], n_x))
+    steps = sorted(range(1, n_line), key=lambda d: -hops(d, n_line))
+
+    def seat_at(dy, dx):
+        other_y, other_x = wrapped(y + dy, n_y), wrapped(x + dx, n_x)
+        hi = jnp.where(other_x >= X_LO, 1, 0)
+        return hi * (n_seats - n_seats // X_HI) + other_y * X_LO + other_x - hi * X_LO
+
     barrier = pltpu.get_barrier_semaphore()
     around = [(dx, dy) for dx in (-1, 0, 1) for dy in (-1, 0, 1) if (dx, dy) != (0, 0)]
-    def greet_plane(d, carry):
-        target = in_plane(wrapped(rank + d, n_plane))
-        pl.semaphore_signal(barrier, inc=1, device_id=target, device_id_type=MESH)
-        return carry
-
-    def greet_line(d, carry):
+    for d in steps:
         target = in_line(wrapped(line + d, n_line))
         pl.semaphore_signal(barrier, inc=1, device_id=target, device_id_type=MESH)
-        return carry
-
-    lax.fori_loop(1, n_line, greet_line, 0)
-    lax.fori_loop(1, n_plane, greet_plane, 0)
+    for chip in chips:
+        for core in range(CORES):
+            if chip != (0, 0):
+                target = in_plane(2 * seat_at(*chip) + core)
+                pl.semaphore_signal(barrier, inc=1, device_id=target, device_id_type=MESH)
+    target = in_plane(2 * seat + 1 - half)
+    pl.semaphore_signal(barrier, inc=1, device_id=target, device_id_type=MESH)
     for dx, dy in around:
         pl.semaphore_signal(barrier, inc=1, device_id=beside(dx, dy), device_id_type=MESH)
     loads = [
@@ -391,23 +408,25 @@
         return remote(src, dst, full_send, full_recv, in_plane(target))
 
     def start_parts(which):
-        def step(d, carry):
-            other = wrapped(seat + d, n_seats)
+        for chip in chips:
+            other = seat_at(*chip)
 
             @pl.when((other < n_busy) & (2 * other + which != rank))
             def _():
                 part_copy(2 * other + which).start()
 
-            return carry
-
-        lax.fori_loop(0, n_seats, step, 0)
-
-    def start_all(make, me, count):
-        def step(d, carry):
-            make(wrapped(me + d, count)).start()
-            return carry
-
-        lax.fori_loop(1, count, step, 0)
+    def start_line():
+        for d in steps:
+            line_copy(wrapped(line + d, n_line)).start()
+
+    def start_full():
+        for chip in chips:
+            other = 2 * seat_at(*chip)
+            for core in range(CORES):
+                if chip == (0, 0):
+                    continue
+                full_copy(other + core).start()
+        full_copy(2 * seat + 1 - half).start()
 
     def whole(ref, count, send, recv):
         part = ref.at[pl.ds(0, count)]
@@ -449,6 +468,7 @@
             value = value + ref[n].astype(F32)
         return value
 
+    copies_b = exchange(turned_b, cells_b, side_b, corner_b, halo_send_b, halo_recv_b)
     offsets = [(kx, ky, kz) for kx in (-1, 0, 1) for ky in (-1, 0, 1) for kz in (-1, 0, 1)]
     for which, own, field, sign in ((0, hidden, 1, -1), (1, delta, 0, 1)):
         sums = kernel_sums(own, cells_a, rim_a, field)
@@ -460,14 +480,13 @@
         packed[pl.ds(top + 7 * C, C), :] = jnp.zeros((C, 128), F32)
         start_parts(which)
 
-    copies_b = exchange(turned_b, cells_b, side_b, corner_b, halo_send_b, halo_recv_b)
 
     @pl.when(busy)
     def _():
         gathered[rank] = share_of(packed, rank)[...]
         part_all.wait_recv()
         column[line] = summed(gathered, n_plane).astype(BF16)
-        start_all(line_copy, line, n_line)
+        start_line()
 
     place_rims(copies_b, cells_b, side_b, corner_b, rim_b)
     pre_two = conv_forward(cells_b, rim_b, band, rim_in, 1) * occupied
@@ -482,7 +501,7 @@
     def _():
         line_all.wait_recv()
         share_of(total, rank)[...] = summed(column, n_line).astype(BF16)
-        start_all(full_copy, rank, n_plane)
+        start_full()
 
     copies_a[1]()
     copies_b[1]()
@@ -502,8 +521,14 @@
 
 
 def deliver(*refs):
-    results, outs, sems = refs[:4], refs[4:8], refs[8:]
-    copies = [pltpu.make_async_copy(*part) for part in zip(results, outs, sems)]
+    results, outs, sems = refs[:4], refs[4:8], refs[8]
+    copies = []
+    for n, (result, out) in enumerate(zip(results, outs)):
+        rows = result.shape[0] // PIECES
+        for piece in range(PIECES):
+            part = pl.ds(piece * rows, rows)
+            sem = sems.at[n, piece]
+            copies.append(pltpu.make_async_copy(result.at[part], out.at[part], sem))
     for copy in copies:
         copy.start()
     for copy in copies:
@@ -570,7 +595,7 @@
         out_shape=out_shape,
         in_specs=[vmem] * 4,
         out_specs=[pl.BlockSpec(memory_space=pl.ANY)] * 4,
-        scratch_shapes=[pltpu.SemaphoreType.DMA] * 4,
+        scratch_shapes=[pltpu.SemaphoreType.DMA((4, PIECES))],
         compiler_params=pltpu.CompilerParams(vmem_limit_bytes=4 * 1024 * 1024),
     )(*[pltpu.with_memory_space_constraint(value, pltpu.VMEM) for value in results])
     flat = (C, SIDE, OWN)

time: 45.1 us -> 43.5 us (0.965)
  Pallas kernels: 44.3 us -> 42.7 us
    pallas_call x1, Pallas kernels: 43.3 us -> 41.6 us  [per_device(): pl.pallas_call(functools.partial(kernel, n_gx, n_gy, factor), out_shape=t...]
where the time goes in v4:
time: 43.5 us; the launch traced here: 43.4 us
  Pallas kernels  42.7 us (98%)
  between operations  0.64 us (1%)
    pallas_call x1, Pallas kernels, per_device(): pl.pallas_call(functools.partial(kernel, n_gx, n_gy, factor), out_shape=t...  41.6 us
    pallas_call x1, Pallas kernels, per_device(): pl.pallas_call(deliver, out_shape=out_shape, in_specs=[vmem] * 4, out_spe...  1.17 us

profile of v4, /device:TPU:1, one launch (start us, length us, event | category | flops | bytes accessed | tf_op | source)
XLA Modules:
  0.0 43.4 jit_solution(4632019517217633347)
XLA Ops:
  0.6 41.6 %shard_map.84 = (bf16[256,384]{1,0:T(8,128)(2,1)S(1)}, bf16[256,384]{1,0:T(8,128)(2,1)S(1)}, f32[864,32]{1,0:T(8,128)S(1)}, f32[864,32]{1,0:T(8,128)S(1)}) custom-call(s32[1,1,6]{2,1,0:T(1,128)} %list_any.1, bf16[256,384]{1,0:T(8,128)(2,1)} %bitcast.10, bf16[256,384]{1,0:T(8,128)(2,1)} %bitcast.11, bf16[864,32]{1,0:T(8,128)(2,1)} %bitcast.8, ...), custom_call_target="tpu_custom_call" | custom-call | tf_op jit(solution)/shard_map/pallas_call | solution.py:564
  42.2 1.2 %shard_map.85 = (bf16[256,384]{1,0:T(8,128)(2,1)}, bf16[256,384]{1,0:T(8,128)(2,1)}, f32[864,32]{1,0:T(8,128)}, f32[864,32]{1,0:T(8,128)}) custom-call(bf16[256,384]{1,0:T(8,128)(2,1)S(1)} %get-tuple-element.12.refs_0_, bf16[256,384]{1,0:T(8,128)(2,1)S(1)} %get-tuple-element.13.refs_1_, f32[864,32]{1,0:T(8,128)S(1)} %get-tuple-element.14.refs_2_, ...), custom_call_target="tpu_custom_call" | custom-call | tf_op jit(solution)/shard_map/pallas_call | solution.py:593

commit v5 on v4

--- a/solution.py
+++ b/solution.py
@@ -17,6 +17,7 @@
 PACKED = 512
 PIECES = 4
 X_HI = 2
+REACH = 3
 X_LO = 2
 CORES = 2
 MESH = pl.DeviceIdType.MESH
@@ -183,7 +184,7 @@
     list_ref, fields_in, weights_in,
     list_sem, f_sem, g_sem, w1_sem, w2_sem,
     halo_send_a, halo_recv_a, halo_send_b, halo_recv_b,
-    part_send, part_recv, line_send, line_recv, full_send, full_recv,
+    part_send, part_recv, line_send, line_recv, full_send, full_recv, hails,
 ):
     gx, gy = lax.axis_index("gx"), lax.axis_index("gy")
     n_line = n_gx // X_HI
@@ -230,18 +231,33 @@
 
     barrier = pltpu.get_barrier_semaphore()
     around = [(dx, dy) for dx in (-1, 0, 1) for dy in (-1, 0, 1) if (dx, dy) != (0, 0)]
-    for d in steps:
-        target = in_line(wrapped(line + d, n_line))
+    far_chips = [chip for chip in chips if hops(chip[0], n_y) + hops(chip[1], n_x) > REACH]
+    far_line = [d for d in steps if hops(d, n_line) > REACH]
+    greeted = [in_line(wrapped(line + d, n_line)) for d in steps if d not in far_line]
+    for chip in chips:
+        if chip not in far_chips and chip != (0, 0):
+            greeted += [in_plane(2 * seat_at(*chip) + core) for core in range(CORES)]
+    greeted.append(in_plane(2 * seat + 1 - half))
+    greeted += [beside(dx, dy) for dx, dy in around]
+    for target in greeted:
         pl.semaphore_signal(barrier, inc=1, device_id=target, device_id_type=MESH)
-    for chip in chips:
-        for core in range(CORES):
-            if chip != (0, 0):
-                target = in_plane(2 * seat_at(*chip) + core)
-                pl.semaphore_signal(barrier, inc=1, device_id=target, device_id_type=MESH)
-    target = in_plane(2 * seat + 1 - half)
-    pl.semaphore_signal(barrier, inc=1, device_id=target, device_id_type=MESH)
-    for dx, dy in around:
-        pl.semaphore_signal(barrier, inc=1, device_id=beside(dx, dy), device_id_type=MESH)
+
+    hailed = [[], []]
+    if far_chips:
+        hailed[0].append(in_plane(2 * seat_at(n_y - 1, 0) + half))
+    if far_line:
+        hailed[0] += [in_line(wrapped(line + d, n_line)) for d in (REACH, -REACH)]
+        rest = n_line // 2 - 2 * REACH
+        hailed[1] += [in_line(wrapped(line + d, n_line)) for d in (rest, -rest)]
+
+    def hail(n):
+        for target in hailed[n]:
+            pl.semaphore_signal(hails.at[n], inc=1, device_id=target, device_id_type=MESH)
+
+    def await_hail(n):
+        if hailed[n]:
+            pl.semaphore_wait(hails.at[n], len(hailed[n]))
+
     loads = [
         pltpu.make_async_copy(src, dst, sem)
         for src, dst, sem in (
@@ -281,7 +297,7 @@
         turned_a[field] = value
         cells_a[field, pl.ds(NZ, OWN), :] = value.T
 
-    pl.semaphore_wait(barrier, len(around) + n_plane - 1 + n_line - 1)
+    pl.semaphore_wait(barrier, len(greeted))
 
     def exchange(turned, cells, side, corner, send, recv):
         low, high = pl.ds(0, C), pl.ds(LANES - C, C)
@@ -365,6 +381,7 @@
         rim[pl.ds(ALL - NZ, NZ), :] = turn(corner[2], corner[3], last_y)[:NZ]
 
     copies_a = exchange(turned_a, cells_a, side_a, corner_a, halo_send_a, halo_recv_a)
+    hail(0)
     for w in range(2):
         loads[3 + w].wait()
         widen_weights(weights_in, quad, w)
@@ -478,8 +495,13 @@
         for n, first in enumerate(range(0, 28, 4)):
             packed[pl.ds(top + n * C, C), :] = fold_four(*parts[first : first + 4])
         packed[pl.ds(top + 7 * C, C), :] = jnp.zeros((C, 128), F32)
+        if which == 0:
+            await_hail(0)
+            hail(1)
         start_parts(which)
 
+
+    await_hail(1)
 
     @pl.when(busy)
     def _():
@@ -585,7 +607,8 @@
         ]
         + [pltpu.SemaphoreType.DMA] * 5
         + [pltpu.SemaphoreType.DMA((3,))] * 4
-        + [pltpu.SemaphoreType.DMA] * 6,
+        + [pltpu.SemaphoreType.DMA] * 6
+        + [pltpu.SemaphoreType.REGULAR((2,))],
         compiler_params=pltpu.CompilerParams(
             collective_id=0, has_side_effects=True, vmem_limit_bytes=40 * 1024 * 1024
         ),

time: 43.5 us -> 42.3 us (0.972)
  Pallas kernels: 42.7 us -> 41.5 us
    pallas_call x1, Pallas kernels: 41.6 us -> 40.3 us  [per_device(): pl.pallas_call(functools.partial(kernel, n_gx, n_gy, factor), out_shape=t...]
where the time goes in v5:
time: 42.3 us; the launch traced here: 42.1 us
  Pallas kernels  41.5 us (98%)
  between operations  0.64 us (2%)
    pallas_call x1, Pallas kernels, per_device(): pl.pallas_call(functools.partial(kernel, n_gx, n_gy, factor), out_shape=t...  40.3 us
    pallas_call x1, Pallas kernels, per_device(): pl.pallas_call(deliver, out_shape=out_shape, in_specs=[vmem] * 4, out_spe...  1.17 us

profile of v5, /device:TPU:1, one launch (start us, length us, event | category | flops | bytes accessed | tf_op | source)
XLA Modules:
  0.0 42.1 jit_solution(7712535077259136815)
XLA Ops:
  0.6 40.3 %shard_map.84 = (bf16[256,384]{1,0:T(8,128)(2,1)S(1)}, bf16[256,384]{1,0:T(8,128)(2,1)S(1)}, f32[864,32]{1,0:T(8,128)S(1)}, f32[864,32]{1,0:T(8,128)S(1)}) custom-call(s32[1,1,6]{2,1,0:T(1,128)} %list_any.1, bf16[256,384]{1,0:T(8,128)(2,1)} %bitcast.10, bf16[256,384]{1,0:T(8,128)(2,1)} %bitcast.11, bf16[864,32]{1,0:T(8,128)(2,1)} %bitcast.8, ...), custom_call_target="tpu_custom_call" | custom-call | tf_op jit(solution)/shard_map/pallas_call | solution.py:586
  41.0 1.2 %shard_map.85 = (bf16[256,384]{1,0:T(8,128)(2,1)}, bf16[256,384]{1,0:T(8,128)(2,1)}, f32[864,32]{1,0:T(8,128)}, f32[864,32]{1,0:T(8,128)}) custom-call(bf16[256,384]{1,0:T(8,128)(2,1)S(1)} %get-tuple-element.12.refs_0_, bf16[256,384]{1,0:T(8,128)(2,1)S(1)} %get-tuple-element.13.refs_1_, f32[864,32]{1,0:T(8,128)S(1)} %get-tuple-element.14.refs_2_, ...), custom_call_target="tpu_custom_call" | custom-call | tf_op jit(solution)/shard_map/pallas_call | solution.py:616

commit v6 on v5

--- a/solution.py
+++ b/solution.py
@@ -134,10 +134,12 @@
     )
     blocks = lane_block()
     sums = {}
+    shifts = [pl.ds(shift * NZ, OWN) for shift in range(3)]
+    mains = dot(tall, jnp.concatenate([cells[field, rows, :] for rows in shifts], axis=1))
+    edges = dot(ends, jnp.concatenate([rim[rows, :] for rows in shifts], axis=1))
     for sy in (-1, 0, 1):
-        rows = pl.ds((1 + sy) * NZ, OWN)
-        main = dot(tall, cells[field, rows, :])
-        edge = dot(ends, rim[rows, :])
+        main = mains[:, (1 + sy) * LANES : (2 + sy) * LANES]
+        edge = edges[:, (1 + sy) * 128 : (2 + sy) * 128]
         for n, sz in enumerate((-1, 0, 1)):
             for sx in (-1, 0, 1):
                 halves = []
@@ -422,7 +424,7 @@
 
     def full_copy(target):
         src, dst = share_of(total, rank), share_of(total, rank)
-        return remote(src, dst, full_send, full_recv, in_plane(target))
+        return remote(src, dst, full_send, full_recv.at[half], in_plane(target))
 
     def start_parts(which):
         for chip in chips:
@@ -467,16 +469,21 @@
             whole(gathered, sent, part_send, part_recv).wait_send,
         )
 
-    def wait_full():
-        landed = 2 * n_busy * share
-        when_busy(
-            whole(total, landed - share, full_send, full_recv).wait_recv,
-            whole(total, landed, full_send, full_recv).wait_recv,
-        )
+    def wait_full(which):
+        landed = n_busy * share
+        mine = busy & (half == which)
+
+        @pl.when(mine)
+        def _():
+            whole(total, landed - share, full_send, full_recv.at[which]).wait_recv()
+
+        @pl.when(jnp.logical_not(mine))
+        def _():
+            whole(total, landed, full_send, full_recv.at[which]).wait_recv()
 
     def wait_full_sent():
         when_busy(
-            whole(total, (n_plane - 1) * share, full_send, full_recv).wait_send, nothing
+            whole(total, (n_plane - 1) * share, full_send, full_recv.at[0]).wait_send, nothing
         )
 
     def summed(ref, count):
@@ -529,16 +536,17 @@
     copies_b[1]()
     wait_parts_sent()
     pl.when(busy)(line_all.wait_send)
-    wait_full()
-
-    for n, first in enumerate(range(0, 27, 4)):
-        count = min(4, 27 - first)
+    groups = [(n, first, min(4, 27 - first)) for n, first in enumerate(range(0, 27, 4))]
+    wait_full(0)
+    for n, first, count in groups:
+        group = total[pl.ds(n * C, C), :].astype(F32) * factor
+        for k in range(count):
+            two_ref[pl.ds((first + k) * C, C), :] = group[:, k * C : (k + 1) * C]
+    wait_full(1)
+    for n, first, count in groups:
         one_ref[pl.ds(first * C, count * C), :] = (
             total[pl.ds(PACKED // 2 + n * C, C), :].astype(F32).T[: count * C] * factor
         )
-        group = total[pl.ds(n * C, C), :].astype(F32) * factor
-        for k in range(count):
-            two_ref[pl.ds((first + k) * C, C), :] = group[:, k * C : (k + 1) * C]
     wait_full_sent()
 
 
@@ -607,7 +615,8 @@
         ]
         + [pltpu.SemaphoreType.DMA] * 5
         + [pltpu.SemaphoreType.DMA((3,))] * 4
-        + [pltpu.SemaphoreType.DMA] * 6
+        + [pltpu.SemaphoreType.DMA] * 5
+        + [pltpu.SemaphoreType.DMA((2,))]
         + [pltpu.SemaphoreType.REGULAR((2,))],
         compiler_params=pltpu.CompilerParams(
             collective_id=0, has_side_effects=True, vmem_limit_bytes=40 * 1024 * 1024

time: 42.3 us -> 42.3 us (level)
  no operation moved by 1% of the time
where the time goes in v6:
time: 42.3 us; the launch traced here: 42.2 us
  Pallas kernels  41.5 us (98%)
  between operations  0.64 us (2%)
    pallas_call x1, Pallas kernels, per_device(): pl.pallas_call(functools.partial(kernel, n_gx, n_gy, factor), out_shape=t...  40.4 us
    pallas_call x1, Pallas kernels, per_device(): pl.pallas_call(deliver, out_shape=out_shape, in_specs=[vmem] * 4, out_spe...  1.17 us

profile of v6, /device:TPU:1, one launch (start us, length us, event | category | flops | bytes accessed | tf_op | source)
XLA Modules:
  0.0 42.2 jit_solution(9204842913492762843)
XLA Ops:
  0.6 40.4 %shard_map.84 = (bf16[256,384]{1,0:T(8,128)(2,1)S(1)}, bf16[256,384]{1,0:T(8,128)(2,1)S(1)}, f32[864,32]{1,0:T(8,128)S(1)}, f32[864,32]{1,0:T(8,128)S(1)}) custom-call(s32[1,1,6]{2,1,0:T(1,128)} %list_any.1, bf16[256,384]{1,0:T(8,128)(2,1)} %bitcast.10, bf16[256,384]{1,0:T(8,128)(2,1)} %bitcast.11, bf16[864,32]{1,0:T(8,128)(2,1)} %bitcast.8, ...), custom_call_target="tpu_custom_call" | custom-call | tf_op jit(solution)/shard_map/pallas_call | solution.py:594
  41.0 1.2 %shard_map.85 = (bf16[256,384]{1,0:T(8,128)(2,1)}, bf16[256,384]{1,0:T(8,128)(2,1)}, f32[864,32]{1,0:T(8,128)}, f32[864,32]{1,0:T(8,128)}) custom-call(bf16[256,384]{1,0:T(8,128)(2,1)S(1)} %get-tuple-element.12.refs_0_, bf16[256,384]{1,0:T(8,128)(2,1)S(1)} %get-tuple-element.13.refs_1_, f32[864,32]{1,0:T(8,128)S(1)} %get-tuple-element.14.refs_2_, ...), custom_call_target="tpu_custom_call" | custom-call | tf_op jit(solution)/shard_map/pallas_call | solution.py:625

commit v7 on v6

--- a/solution.py
+++ b/solution.py
@@ -235,12 +235,13 @@
     around = [(dx, dy) for dx in (-1, 0, 1) for dy in (-1, 0, 1) if (dx, dy) != (0, 0)]
     far_chips = [chip for chip in chips if hops(chip[0], n_y) + hops(chip[1], n_x) > REACH]
     far_line = [d for d in steps if hops(d, n_line) > REACH]
-    greeted = [in_line(wrapped(line + d, n_line)) for d in steps if d not in far_line]
+    around.sort(key=lambda step: -abs(step[0]) - abs(step[1]))
+    greeted = [beside(dx, dy) for dx, dy in around]
+    greeted += [in_line(wrapped(line + d, n_line)) for d in steps if d not in far_line]
     for chip in chips:
         if chip not in far_chips and chip != (0, 0):
             greeted += [in_plane(2 * seat_at(*chip) + core) for core in range(CORES)]
     greeted.append(in_plane(2 * seat + 1 - half))
-    greeted += [beside(dx, dy) for dx, dy in around]
     for target in greeted:
         pl.semaphore_signal(barrier, inc=1, device_id=target, device_id_type=MESH)
 

time: 42.3 us -> 42.3 us (level)
  no operation moved by 1% of the time
where the time goes in v7:
time: 42.3 us; the launch traced here: 42.2 us
  Pallas kernels  41.5 us (98%)
  between operations  0.64 us (2%)
    pallas_call x1, Pallas kernels, per_device(): pl.pallas_call(functools.partial(kernel, n_gx, n_gy, factor), out_shape=t...  40.4 us
    pallas_call x1, Pallas kernels, per_device(): pl.pallas_call(deliver, out_shape=out_shape, in_specs=[vmem] * 4, out_spe...  1.17 us

profile of v7, /device:TPU:1, one launch (start us, length us, event | category | flops | bytes accessed | tf_op | source)
XLA Modules:
  0.0 42.2 jit_solution(2312549129867745839)
XLA Ops:
  0.6 40.4 %shard_map.84 = (bf16[256,384]{1,0:T(8,128)(2,1)S(1)}, bf16[256,384]{1,0:T(8,128)(2,1)S(1)}, f32[864,32]{1,0:T(8,128)S(1)}, f32[864,32]{1,0:T(8,128)S(1)}) custom-call(s32[1,1,6]{2,1,0:T(1,128)} %list_any.1, bf16[256,384]{1,0:T(8,128)(2,1)} %bitcast.10, bf16[256,384]{1,0:T(8,128)(2,1)} %bitcast.11, bf16[864,32]{1,0:T(8,128)(2,1)} %bitcast.8, ...), custom_call_target="tpu_custom_call" | custom-call | tf_op jit(solution)/shard_map/pallas_call | solution.py:595
  41.0 1.2 %shard_map.85 = (bf16[256,384]{1,0:T(8,128)(2,1)}, bf16[256,384]{1,0:T(8,128)(2,1)}, f32[864,32]{1,0:T(8,128)}, f32[864,32]{1,0:T(8,128)}) custom-call(bf16[256,384]{1,0:T(8,128)(2,1)S(1)} %get-tuple-element.12.refs_0_, bf16[256,384]{1,0:T(8,128)(2,1)S(1)} %get-tuple-element.13.refs_1_, f32[864,32]{1,0:T(8,128)S(1)} %get-tuple-element.14.refs_2_, ...), custom_call_target="tpu_custom_call" | custom-call | tf_op jit(solution)/shard_map/pallas_call | solution.py:626
